TPU v7x, 32 devices: a whole 2x2x4 slice. The times are simulated.
32 devices in a mesh: dp: 4 (over x, core), space: 8 (over z, y).
Axes of the slice: x: 2, y: 2, z: 4, core: 2. Of those that a mesh axis runs over, the one named last changes fastest.
Arguments:
- features: bfloat16 [4, 32, 256, 512], P('dp', None, 'space'), may hold values from -6 to 6
- cotangent: bfloat16 [4, 32, 256, 512], P('dp', None, 'space'), may hold values from -6 to 6
- conv_kernel: float32 [7, 7, 512], replicated, may hold values from -0.875 to 0.875
- conv_bias: float32 [512], replicated, may hold values from -3 to 3
- norm_gain: float32 [512], replicated, may hold values from 0.5 to 1.5
- norm_bias: float32 [512], replicated, may hold values from -3 to 3
- weight_in: bfloat16 [512, 2048], P(('dp', 'space')), may hold values from -0.25 to 0.25
- bias_in: float32 [2048], replicated, may hold values from -3 to 3
- weight_out: bfloat16 [2048, 512], P(('dp', 'space')), may hold values from -0.125 to 0.125
- bias_out: float32 [512], replicated, may hold values from -3 to 3
- layer_scale: float32 [512], replicated, may hold values from 0.3 to 1.5
Outputs:
- block_out: bfloat16 [4, 32, 256, 512], P('dp', None, 'space')
- grad_features: bfloat16 [4, 32, 256, 512], P('dp', None, 'space')
- grad_kernel: float32 [7, 7, 512], replicated
- grad_convbias: float32 [512], replicated
- grad_gain: float32 [512], replicated
- grad_normbias: float32 [512], replicated
- grad_inproj: float32 [512, 2048], P(('dp', 'space'))
- grad_inbias: float32 [2048], replicated
- grad_outproj: float32 [2048, 512], P(('dp', 'space'))
- grad_outbias: float32 [512], replicated
- grad_scale: float32 [512], replicated
All inputs are finite; a program needn't handle non-finite values.
Results may differ from a plain program's by a relative error of at most 0.009.
Values may be sent and summed in bfloat16 or wider, within the bound.
A program may use at most 576 MiB of HBM per device.

v0:
```python
import jax
import jax.numpy as jnp
from jax import lax
from jax.sharding import PartitionSpec as P

KS = 7


NORM_EPS = 1e-06


def padded_2(x, sides, width):
    for axis, dim in sides:
        peers, length = (lax.axis_size(axis), x.shape[dim])
        up = [(i, (i + 1) % peers) for i in range(peers - 1)]
        down = [(j, i) for i, j in up]
        last = lax.slice_in_dim(x, length - width, length, axis=dim)
        initial = lax.slice_in_dim(x, 0, width, axis=dim)
        before = lax.ppermute(last, axis, up)
        after = lax.ppermute(initial, axis, down)
        x = jnp.concatenate([before, x, after], axis=dim)
    return x


def gelu_exact(inputs):
    return jax.nn.gelu(inputs, approximate=False)


def conv_forward(padded, kernel, offset, row_count, col_count):
    summed = jnp.zeros((row_count, col_count, padded.shape[2]), jnp.float32)
    for tap_row in range(KS):
        for tap_col in range(KS):
            window = padded[tap_row : tap_row + row_count, tap_col : tap_col + col_count].astype(
                jnp.float32
            )
            summed = summed + kernel[tap_row, tap_col] * window
    return (summed + offset).astype(jnp.bfloat16)


def conv_backward(grad_padded, kernel, row_count, col_count):
    summed = jnp.zeros((row_count, col_count, grad_padded.shape[2]), jnp.float32)
    for tap_row in range(KS):
        for tap_col in range(KS):
            row_start = KS - 1 - tap_row
            col_start = KS - 1 - tap_col
            window = grad_padded[
                row_start : row_start + row_count, col_start : col_start + col_count
            ].astype(jnp.float32)
            summed = summed + kernel[tap_row, tap_col] * window
    return summed


def kernel_gradient(grad_conv, padded, row_count, col_count):
    grad_wide = grad_conv.astype(jnp.float32)
    taps = []
    for tap_row in range(KS):
        tap_line = []
        for tap_col in range(KS):
            window = padded[tap_row : tap_row + row_count, tap_col : tap_col + col_count].astype(
                jnp.float32
            )
            tap_line.append(jnp.sum(grad_wide * window, axis=(0, 1)))
        taps.append(jnp.stack(tap_line))
    return jnp.stack(taps)


def norm_mlp(
    conv_out,
    source,
    upstream,
    norm_gain,
    norm_bias,
    weight_in,
    bias_in,
    weight_out,
    bias_out,
    layer_scale,
):
    widened = conv_out.astype(jnp.float32)
    center = jnp.mean(widened, axis=-1, keepdims=True)
    shifted = widened - center
    inv_std = lax.rsqrt(jnp.mean(shifted * shifted, axis=-1, keepdims=True) + NORM_EPS)
    normed = shifted * inv_std
    activated = (normed * norm_gain + norm_bias).astype(jnp.bfloat16)
    pre_act = jnp.dot(activated, weight_in, preferred_element_type=jnp.float32) + bias_in
    hidden_wide, gelu_back = jax.vjp(gelu_exact, pre_act)
    hidden = hidden_wide.astype(jnp.bfloat16)
    branch = jnp.dot(hidden, weight_out, preferred_element_type=jnp.float32) + bias_out
    block_out = (source.astype(jnp.float32) + layer_scale * branch).astype(jnp.bfloat16)
    upstream_wide = upstream.astype(jnp.float32)
    d_branch = layer_scale * upstream_wide
    d_branch_b = d_branch.astype(jnp.bfloat16)
    grad_scale = jnp.sum(upstream_wide * branch, axis=0)
    grad_outbias = jnp.sum(d_branch, axis=0)
    grad_outproj = lax.dot_general(
        hidden, d_branch_b, (((0,), (0,)), ((), ())), preferred_element_type=jnp.float32
    )
    d_hidden = lax.dot_general(
        d_branch_b, weight_out, (((1,), (1,)), ((), ())), preferred_element_type=jnp.float32
    )
    d_pre = gelu_back(d_hidden)[0]
    d_pre_b = d_pre.astype(jnp.bfloat16)
    grad_inbias = jnp.sum(d_pre, axis=0)
    grad_inproj = lax.dot_general(
        activated, d_pre_b, (((0,), (0,)), ((), ())), preferred_element_type=jnp.float32
    )
    d_act = lax.dot_general(
        d_pre_b, weight_in, (((1,), (1,)), ((), ())), preferred_element_type=jnp.float32
    )
    grad_gain = jnp.sum(d_act * normed, axis=0)
    grad_normbias = jnp.sum(d_act, axis=0)
    scaled = d_act * norm_gain
    grad_conv = inv_std * (
        scaled
        - jnp.mean(scaled, axis=-1, keepdims=True)
        - normed * jnp.mean(scaled * normed, axis=-1, keepdims=True)
    )
    return (
        block_out,
        grad_conv.astype(jnp.bfloat16),
        (
            grad_gain,
            grad_normbias,
            grad_inproj,
            grad_inbias,
            grad_outproj,
            grad_outbias,
            grad_scale,
        ),
    )


def local(
    features,
    cotangent,
    conv_kernel,
    conv_bias,
    norm_gain,
    norm_bias,
    weight_in,
    bias_in,
    weight_out,
    bias_out,
    layer_scale,
):
    reach = KS // 2
    source = features[0]
    upstream = cotangent[0]
    row_count, col_count, channels = source.shape
    full_in, full_out = (
        lax.all_gather(weight_in, ("dp", "space"), axis=0, tiled=True),
        lax.all_gather(weight_out, ("dp", "space"), axis=0, tiled=True),
    )
    rimmed = padded_2(source, (("space", 1),), reach)
    padded = jnp.pad(rimmed, ((reach, reach), (0, 0), (0, 0)))
    conv_out = conv_forward(padded, conv_kernel, conv_bias, row_count, col_count)
    block_out, grad_conv, partials = norm_mlp(
        conv_out.reshape(-1, channels),
        source.reshape(-1, channels),
        upstream.reshape(-1, channels),
        norm_gain,
        norm_bias,
        full_in,
        bias_in,
        full_out,
        bias_out,
        layer_scale,
    )
    grad_conv = grad_conv.reshape(row_count, col_count, channels)
    grad_rimmed = padded_2(grad_conv, (("space", 1),), reach)
    grad_padded = jnp.pad(grad_rimmed, ((reach, reach), (0, 0), (0, 0)))
    conv_back = conv_backward(grad_padded, conv_kernel, row_count, col_count)
    grad_kern = kernel_gradient(grad_conv, padded, row_count, col_count)
    grad_cbias = jnp.sum(grad_conv.astype(jnp.float32), axis=(0, 1))
    grad_feat = (upstream.astype(jnp.float32) + conv_back).astype(jnp.bfloat16)
    grad_gain, grad_normbias, grad_inproj, grad_inbias, grad_outproj, grad_outbias, grad_scale = (
        partials
    )
    reduced = lax.psum(
        (grad_kern, grad_cbias, grad_gain, grad_normbias, grad_inbias, grad_outbias, grad_scale),
        ("dp", "space"),
    )
    owned_in, owned_out = (
        lax.psum_scatter(grad_inproj, ("dp", "space"), scatter_dimension=0, tiled=True),
        lax.psum_scatter(grad_outproj, ("dp", "space"), scatter_dimension=0, tiled=True),
    )
    return (
        block_out.reshape(1, row_count, col_count, channels),
        grad_feat[None],
        reduced[0],
        reduced[1],
        reduced[2],
        reduced[3],
        owned_in,
        reduced[4],
        owned_out,
        reduced[5],
        reduced[6],
    )


def solution(mesh):
    return jax.shard_map(
        local,
        mesh=mesh,
        in_specs=(
            P("dp", None, "space", None),
            P("dp", None, "space", None),
            P(),
            P(),
            P(),
            P(),
            P(("dp", "space"), None),
            P(),
            P(("dp", "space"), None),
            P(),
            P(),
        ),
        out_specs=(
            P("dp", None, "space", None),
            P("dp", None, "space", None),
            P(),
            P(),
            P(),
            P(),
            P(("dp", "space"), None),
            P(),
            P(("dp", "space"), None),
            P(),
            P(),
        ),
        check_vma=False,
    )
```

profile of v0, /device:TPU:0, one launch (start us, length us, event | category | flops | bytes accessed | tf_op | source)
XLA Modules:
  0.0 583.8 jit_solution(10404483312146317047)
XLA Ops:
  9.1 4.9 collective-permute-start
  18.6 2.3 collective-permute-done.1
  20.9 2.0 select_maximum_fusion.2
  22.9 16.5 %convert_reduce_fusion.1 = (f32[32,32]{1,0:T(8,128)S(1)}, bf16[32,32,512]{2,1,0:T(8,128)(2,1)}) fusion(f32[512]{0:T(512)S(1)} %copy-done.8, bf16[38,38,512]{2,1,0:T(8,128)(2,1)S(1)} %select_maximum_fusion.2, f32[512]{0:T(512)S(1)} %bitcast.310, f32[512]{0:T(512)S(1)} %bitcast.312, f32[512]{0:T(512)S(1)} %bitcast.218, f32[512]{0:T(512)S(1)} %bitcast.220, ...), kind=kLoop, calls=%fused_computation.278 | loop fusion | flops 88079360 | bytes 46440448 | tf_op jit(solution)/shard_map/reduce_sum | solution.py:80
  39.5 1.7 multiply_reduce_fusion.2
  41.3 2.7 add_convert_fusion
  44.1 26.3 %all-gather.3.cloned.1.call-done = bf16[512,2048]{1,0:T(8,128)(2,1)} async-done(((bf16[16,2048]{1,0:T(8,128)(2,1)}), bf16[512,2048]{1,0:T(8,128)(2,1)}) %all-gather.3.cloned.1.call-update) | async-done | bytes 2097168 | tf_op jit(solution)/shard_map/all_gather | solution.py:151
  70.3 23.4 %multiply_convert_fusion = (bf16[1024,2048]{1,0:T(8,128)(2,1)}, f32[1024,2048]{1,0:T(8,128)}, f32[1024,2048]{1,0:T(8,128)}) fusion(f32[2048]{0:T(1024)S(1)} %copy-done.13, bf16[1024,512]{1,0:T(8,128)(2,1)} %add_convert_fusion, bf16[512,2048]{1,0:T(8,128)(2,1)} %all-gather.3.cloned.1.call-done), kind=kOutput, calls=%fused_computation.52 | convolution fusion | flops 2285895680 | bytes 24125440 | tf_op jit(solution)/shard_map/dot_general | solution.py:85
  93.7 35.0 %all-gather.5.cloned.1.call-done = bf16[2048,512]{1,0:T(8,128)(2,1)} async-done(((bf16[64,512]{1,0:T(8,128)(2,1)}), bf16[2048,512]{1,0:T(8,128)(2,1)}) %all-gather.5.cloned.1.call-update) | async-done | bytes 2097168 | tf_op jit(solution)/shard_map/all_gather | solution.py:152
  128.7 6.9 %fusion.134 = (f32[512]{0:T(512)S(1)}, bf16[1024,512]{1,0:T(8,128)(2,1)}, bf16[1024,512]{1,0:T(8,128)(2,1)S(1)}) fusion(bf16[1,32,32,512]{3,2,1,0:T(8,128)(2,1)} %param.12, f32[512]{0:T(512)S(1)} %copy-done.14, f32[512]{0:T(512)S(1)} %copy-done.9, bf16[1,32,32,512]{3,2,1,0:T(8,128)(2,1)S(1)} %copy-done, bf16[1024,2048]{1,0:T(8,128)(2,1)} %get-tuple-element.81, ...), kind=kOutput, calls=%fused_computation.251 | convolution fusion | flops 2152726016 | bytes 10491904 | tf_op jit(solution)/shard_map/dot_general | solution.py:88
  135.6 8.0 %fusion.156 = (f32[2048]{0:T(1024)S(1)}, bf16[1024,2048]{1,0:T(8,128)(2,1)S(1)}) fusion(f32[1024,2048]{1,0:T(8,128)S(1)} %copy-done.16, bf16[1024,512]{1,0:T(8,128)(2,1)S(1)} %get-tuple-element.87, bf16[2048,512]{1,0:T(8,128)(2,1)S(1)} %copy-done.12, f32[1024,2048]{1,0:T(8,128)} %get-tuple-element.141, f32[2048]{0:T(1024)S(1)} %copy-done.13), kind=kOutput, calls=%fused_computation.316 | convolution fusion | flops 2181036032 | bytes 24133632 | tf_op jit(solution)/shard_map/dot_general | solution.py:98
  143.7 2.9 multiply_reduce_fusion
  146.6 6.6 %fusion.129 = (f32[512]{0:T(512)S(1)}, f32[512]{0:T(512)S(1)}, f32[512]{0:T(512)S(1)}, f32[512]{0:T(512)S(1)}, f32[512]{0:T(512)S(1)}, /*index=5*/f32[512]{0:T(5...) fusion(bf16[38,38,512]{2,1,0:T(8,128)(2,1)S(1)} %select_maximum, ...), kind=kLoop, calls=%fused_computation.242 | loop fusion | flops 33545216 | bytes 23123968 | tf_op jit(solution)/shard_map/reduce_sum | solution.py:62
  153.6 5.2 fusion.111
  158.8 4.2 fusion.108
  164.3 6.8 %fusion.157 = f32[2048,512]{1,0:T(8,128)} fusion(bf16[1024,2048]{1,0:T(8,128)(2,1)} %get-tuple-element.81, bf16[1024,512]{1,0:T(8,128)(2,1)} %copy-done.15), kind=kOutput, calls=%fused_computation.317 | convolution fusion | flops 2147483648 | bytes 9437184 | tf_op jit(solution)/shard_map/dot_general | solution.py:95
  172.4 6.6 %fusion.136 = f32[512,2048]{1,0:T(8,128)} fusion(bf16[1024,512]{1,0:T(8,128)(2,1)S(1)} %copy-done.4, bf16[1024,2048]{1,0:T(8,128)(2,1)} %copy-done.3), kind=kOutput, calls=%fused_computation.257 | convolution fusion | flops 2147483648 | bytes 9437184 | tf_op jit(solution)/shard_map/dot_general | solution.py:104
  179.1 3.5 collective-permute-start.2
  184.2 41.0 %all-reduce.2 = (f32[512]{0:T(512)}, f32[512]{0:T(512)}, f32[512]{0:T(512)}, f32[2048]{0:T(1024)}, f32[512]{0:T(512)}, /*index=5*/f32[512]{0:T(512)}) all-reduce(f32[512]{0:T(512)S(1)} %get-tuple-element.66, f32[512]{0:T(512)S(1)} %get-tuple-element.11, ...), channel_id=1, replica_groups=mesh['dp'=4,'space'=8] {'dp','space'}, use_global_device_ids=true, to_apply=%region_55.56 | all-reduce | flops 4608 | bytes 36864 | tf_op jit(solution)/shard_map/psum | solution.py:179
  226.0 16.7 %fusion.149 = bf16[1,32,32,512]{3,2,1,0:T(8,128)(2,1)} fusion(bf16[38,38,512]{2,1,0:T(8,128)(2,1)S(1)} %select_maximum_fusion, f32[512]{0:T(512)S(1)} %bitcast.311, f32[512]{0:T(512)S(1)} %bitcast.313, f32[512]{0:T(512)S(1)} %bitcast.219, f32[512]{0:T(512)S(1)} %bitcast.221, f32[512]{0:T(512)S(1)} %bitcast.223, f32[512]{0:T(512)S(1)} %bitcast.225, ...), kind=kLoop, calls=%fused_computation.299 | loop fusion | flops 87556096 | bytes 47482880 | tf_op jit(solution)/shard_map/broadcast_in_dim | solution.py:189
  242.7 41.1 %all-reduce.5.cloned.1.call-done = f32[7,7,512]{2,1,0:T(8,128)} async-done(((f32[7,7,512]{2,1,0:T(8,128)}), f32[7,7,512]{2,1,0:T(8,128)}) %all-reduce.5.cloned.1.call-update) | async-done | bytes 100368 | tf_op jit(solution)/shard_map/psum | solution.py:179
  283.8 147.9 %reduce-scatter.5.cloned.1.call-done = f32[64,512]{1,0:T(8,128)} async-done(((f32[2048,512]{1,0:T(8,128)}), f32[64,512]{1,0:T(8,128)}) %reduce-scatter.5.cloned.1.call-update) | async-done | bytes 131088 | tf_op jit(solution)/shard_map/reduce_scatter | solution.py:185
  431.7 144.1 %reduce-scatter.3.cloned.1.call-done = f32[16,2048]{1,0:T(8,128)} async-done(((f32[512,2048]{1,0:T(8,128)}), f32[16,2048]{1,0:T(8,128)}) %reduce-scatter.3.cloned.1.call-update) | async-done | bytes 131088 | tf_op jit(solution)/shard_map/reduce_scatter | solution.py:184
  575.8 1.6 copy.29
  (76 shorter events, 12.1 us)
Async XLA Ops:
  7.2 15.7 %copy-start = (bf16[1,32,32,512]{3,2,1,0:T(8,128)(2,1)S(1)}, bf16[1,32,32,512]{3,2,1,0:T(8,128)(2,1)}, u32[]{:S(2)}) copy-start(bf16[1,32,32,512]{3,2,1,0:T(8,128)(2,1)} %param.11) | copy-start | bytes 3145732
  7.2 15.7 %copy-start.8 = (f32[512]{0:T(512)S(1)}, f32[512]{0:T(512)}, u32[]{:S(2)}) copy-start(f32[512]{0:T(512)} %param.14) | copy-start | bytes 6148
  7.2 63.1 %all-gather.3.cloned.1.call-start = ((), (), s32[]{:S(2)}) async-start(), calls=%async_computation.2 | async-start | bytes 2162688 | tf_op jit(solution)/shard_map/all_gather | solution.py:151
  7.9 120.8 %all-gather.5.cloned.1.call-start = ((), (), s32[]{:S(2)}) async-start(), calls=%async_computation.3 | async-start | bytes 2162688 | tf_op jit(solution)/shard_map/all_gather | solution.py:152
  9.1 9.5 %collective-permute-start = (bf16[32,3,512]{2,1,0:T(4,128)(2,1)S(1)}, bf16[32,3,512]{2,1,0:T(4,128)(2,1)S(1)}, u32[]{:S(2)}, u32[]{:S(2)}) collective-permute-start(bf16[32,3,512]{2,1,0:T(4,128)(2,1)S(1)} %get-tuple-element.90), channel_id=1, source_target_pairs={{0,1},{1,2},{2,3},{3,4},{4,5},{5,6},{6,7},{8,9},{9,10},{10,11},{11... | collective-permute-start | bytes 294920 | tf_op jit(solution)/shard_map/ppermute | solution.py:19
  14.0 6.9 %collective-permute-start.1 = (bf16[32,3,512]{2,1,0:T(4,128)(2,1)S(1)}, bf16[32,3,512]{2,1,0:T(4,128)(2,1)S(1)}, u32[]{:S(2)}, u32[]{:S(2)}) collective-permute-start(bf16[32,3,512]{2,1,0:T(4,128)(2,1)S(1)} %get-tuple-element.91), channel_id=1, source_target_pairs={{1,0},{2,1},{3,2},{4,3},{5,4},{6,5},{7,6},{9,8},{10,9},{11,10},{12... | collective-permute-start | bytes 294920 | tf_op jit(solution)/shard_map/ppermute | solution.py:20
  15.3 268.5 %all-reduce.5.cloned.1.call-start = ((), (), s32[]{:S(2)}) async-start(), calls=%async_computation.4 | async-start | bytes 229376 | tf_op jit(solution)/shard_map/psum | solution.py:179
  22.9 18.4 %copy-start.7 = (f32[512]{0:T(512)S(1)}, f32[512]{0:T(512)}, u32[]{:S(2)}) copy-start(f32[512]{0:T(512)} %param.15) | copy-start | bytes 6148
  22.9 18.4 %copy-start.10 = (f32[512]{0:T(512)S(1)}, f32[512]{0:T(512)}, u32[]{:S(2)}) copy-start(f32[512]{0:T(512)} %param.16) | copy-start | bytes 6148
  39.4 30.9 %copy-start.13 = (f32[2048]{0:T(1024)S(1)}, f32[2048]{0:T(1024)}, u32[]{:S(2)}) copy-start(f32[2048]{0:T(1024)} %param.18) | copy-start | bytes 24580
  44.1 84.7 %copy-start.9 = (f32[512]{0:T(512)S(1)}, f32[512]{0:T(512)}, u32[]{:S(2)}) copy-start(f32[512]{0:T(512)} %param.21) | copy-start | bytes 6148
  44.1 84.7 %copy-start.14 = (f32[512]{0:T(512)S(1)}, f32[512]{0:T(512)}, u32[]{:S(2)}) copy-start(f32[512]{0:T(512)} %param.20) | copy-start | bytes 6148
  128.7 6.9 %copy-start.12 = (bf16[2048,512]{1,0:T(8,128)(2,1)S(1)}, bf16[2048,512]{1,0:T(8,128)(2,1)}, u32[]{:S(2)}) copy-start(bf16[2048,512]{1,0:T(8,128)(2,1)} %all-gather.5.cloned.1.call-done) | copy-start | bytes 6291460
  128.7 6.9 %copy-start.16 = (f32[1024,2048]{1,0:T(8,128)S(1)}, f32[1024,2048]{1,0:T(8,128)}, u32[]{:S(2)}) copy-start(f32[1024,2048]{1,0:T(8,128)} %get-tuple-element.82) | copy-start | bytes 25165828
  135.6 8.0 %copy-start.15 = (bf16[1024,512]{1,0:T(8,128)(2,1)}, bf16[1024,512]{1,0:T(8,128)(2,1)S(1)}, u32[]{:S(2)}) copy-start(bf16[1024,512]{1,0:T(8,128)(2,1)S(1)} %get-tuple-element.87) | copy-start | bytes 3145732
  135.6 8.0 %copy-start.2 = (bf16[32,32,512]{2,1,0:T(8,128)(2,1)S(1)}, bf16[32,32,512]{2,1,0:T(8,128)(2,1)}, u32[]{:S(2)}) copy-start(bf16[32,32,512]{2,1,0:T(8,128)(2,1)} %get-tuple-element.84) | copy-start | bytes 3145732
  135.6 8.0 %copy-start.11 = (bf16[512,2048]{1,0:T(8,128)(2,1)S(1)}, bf16[512,2048]{1,0:T(8,128)(2,1)}, u32[]{:S(2)}) copy-start(bf16[512,2048]{1,0:T(8,128)(2,1)} %all-gather.3.cloned.1.call-done) | copy-start | bytes 6291460
  143.6 2.9 copy-start.3
  146.5 6.6 %copy-start.1 = (bf16[1,32,32,512]{3,2,1,0:T(8,128)(2,1)S(1)}, bf16[1,32,32,512]{3,2,1,0:T(8,128)(2,1)}, u32[]{:S(2)}) copy-start(bf16[1,32,32,512]{3,2,1,0:T(8,128)(2,1)} %param.11) | copy-start | bytes 3145732
  164.0 267.6 %reduce-scatter.5.cloned.1.call-start = ((), (), s32[]{:S(2)}) async-start(), calls=%async_computation.6 | async-start | bytes 4325376 | tf_op jit(solution)/shard_map/reduce_scatter | solution.py:185
  171.2 404.6 %reduce-scatter.3.cloned.1.call-start = ((), (), s32[]{:S(2)}) async-start(), calls=%async_computation.5 | async-start | bytes 4325376 | tf_op jit(solution)/shard_map/reduce_scatter | solution.py:184
  178.9 4.9 copy-start.5
  179.1 46.1 %collective-permute-start.2 = (bf16[32,3,512]{2,1,0:T(4,128)(2,1)S(1)}, bf16[32,3,512]{2,1,0:T(4,128)(2,1)S(1)}, u32[]{:S(2)}, u32[]{:S(2)}) collective-permute-start(bf16[32,3,512]{2,1,0:T(4,128)(2,1)S(1)} %get-tuple-element.88), channel_id=1, source_target_pairs={{0,1},{1,2},{2,3},{3,4},{4,5},{5,6},{6,7},{8,9},{9,10},{10,11},{11... | collective-permute-start | bytes 294920 | tf_op jit(solution)/shard_map/ppermute | solution.py:19
  182.6 42.6 %collective-permute-start.3 = (bf16[32,3,512]{2,1,0:T(4,128)(2,1)S(1)}, bf16[32,3,512]{2,1,0:T(4,128)(2,1)S(1)}, u32[]{:S(2)}, u32[]{:S(2)}) collective-permute-start(bf16[32,3,512]{2,1,0:T(4,128)(2,1)S(1)} %get-tuple-element.89), channel_id=1, source_target_pairs={{1,0},{2,1},{3,2},{4,3},{5,4},{6,5},{7,6},{9,8},{10,9},{11,10},{12... | collective-permute-start | bytes 294920 | tf_op jit(solution)/shard_map/ppermute | solution.py:20
  (2 other events, 1.9 us)
Sparse Core Ops, SparseCore 0:
  11.0 59.2 all-gather.2
  73.3 55.3 all-gather.4
  164.2 119.5 all-reduce.4
  286.5 145.1 reduce-scatter.4
  434.4 141.3 reduce-scatter.2
where the time goes:
time: 585 us; the launch traced here: 584 us
  waiting for transfers between devices  397 us (68%)
  other arithmetic  57.2 us (10%)
  matrix products  54.5 us (9%)
  blocking collectives  41 us (7%)
  between operations  14.1 us (2%)
  starting transfers between devices  11.4 us (2%)
  local copies, waits for them, and re-layouts  8.29 us (1%)
    reduce_scatter x1, waiting for transfers between devices, local(): lax.psum_scatter(grad_outproj, ('dp', 'space'), scatter_dimension=0, tile...  148 us
    reduce_scatter x1, waiting for transfers between devices, local(): lax.psum_scatter(grad_inproj, ('dp', 'space'), scatter_dimension=0, tiled...  144 us
    psum x1, waiting for transfers between devices, local(): lax.psum((grad_kern, grad_cbias, grad_gain, grad_normbias, grad_inbias, g...  41.1 us
    psum x1, blocking collectives, local(): lax.psum((grad_kern, grad_cbias, grad_gain, grad_normbias, grad_inbias, g...  41 us
    all_gather x1, waiting for transfers between devices, local(): lax.all_gather(weight_out, ('dp', 'space'), axis=0, tiled=True)  35 us
    all_gather x1, waiting for transfers between devices, local(): lax.all_gather(weight_in, ('dp', 'space'), axis=0, tiled=True)  26.3 us
    dot_general x1, matrix products, norm_mlp(): jnp.dot(activated, weight_in, preferred_element_type=jnp.float32) + bias_in  23.4 us
    broadcast_in_dim x1, other arithmetic, local(): grad_feat[None]  16.7 us
  transfers between devices with their start and end apart: 9, of which 6 were waited for; matrix products, arithmetic and copies ran while one was open for 14% of the time, Pallas kernels for 0%

commit v1 on v0

--- a/solution.py
+++ b/solution.py
@@ -20,6 +20,67 @@
         after = lax.ppermute(initial, axis, down)
         x = jnp.concatenate([before, x, after], axis=dim)
     return x
+
+
+def index_bits():
+    listed = []
+    for axis in ("dp", "space"):
+        stride = 1
+        while stride < lax.axis_size(axis):
+            listed.append((axis, stride))
+            stride *= 2
+    return listed
+
+
+def row_order(key):
+    return (key[0] != "dp", -key[1])
+
+
+def swapped(x, key):
+    axis, stride = key
+    return lax.ppermute(x, axis, [(i, i ^ stride) for i in range(lax.axis_size(axis))])
+
+
+def own_bit(key):
+    return (lax.axis_index(key[0]) // key[1]) % 2
+
+
+def gather_rows(x):
+    tail = x.shape[1]
+    present = []
+    for key in index_bits()[::-1]:
+        other = swapped(x, key)
+        present = sorted(present + [key], key=row_order)
+        at = present.index(key)
+        high = own_bit(key) == 1
+        x = jnp.stack([jnp.where(high, other, x), jnp.where(high, x, other)], axis=at)
+    return x.reshape(-1, tail)
+
+
+def scatter_sum_rows(x):
+    keys = index_bits()
+    present = sorted(keys, key=row_order)
+    x = x.reshape((2,) * len(keys) + (-1, x.shape[1]))
+    for key in keys:
+        at = present.index(key)
+        bit = own_bit(key)
+        kept = lax.dynamic_index_in_dim(x, bit, at, keepdims=False)
+        sent = lax.dynamic_index_in_dim(x, 1 - bit, at, keepdims=False).astype(jnp.bfloat16)
+        x = kept + swapped(sent, key).astype(jnp.float32)
+        present.remove(key)
+    return x
+
+
+def sum_everywhere(parts):
+    flat = jnp.concatenate([part.reshape(-1, parts[0].shape[-1]) for part in parts])
+    for key in index_bits():
+        flat = flat + swapped(flat, key)
+    outs, at = [], 0
+    for part in parts:
+        rows = part.size // flat.shape[1]
+        outs.append(flat[at : at + rows].reshape(part.shape))
+        at += rows
+    return outs
 
 
 def gelu_exact(inputs):
@@ -148,8 +209,8 @@
     upstream = cotangent[0]
     row_count, col_count, channels = source.shape
     full_in, full_out = (
-        lax.all_gather(weight_in, ("dp", "space"), axis=0, tiled=True),
-        lax.all_gather(weight_out, ("dp", "space"), axis=0, tiled=True),
+        gather_rows(weight_in),
+        gather_rows(weight_out),
     )
     rimmed = padded_2(source, (("space", 1),), reach)
     padded = jnp.pad(rimmed, ((reach, reach), (0, 0), (0, 0)))
@@ -176,14 +237,10 @@
     grad_gain, grad_normbias, grad_inproj, grad_inbias, grad_outproj, grad_outbias, grad_scale = (
         partials
     )
-    reduced = lax.psum(
-        (grad_kern, grad_cbias, grad_gain, grad_normbias, grad_inbias, grad_outbias, grad_scale),
-        ("dp", "space"),
-    )
-    owned_in, owned_out = (
-        lax.psum_scatter(grad_inproj, ("dp", "space"), scatter_dimension=0, tiled=True),
-        lax.psum_scatter(grad_outproj, ("dp", "space"), scatter_dimension=0, tiled=True),
-    )
+    early = sum_everywhere((grad_gain, grad_normbias, grad_inbias, grad_outbias, grad_scale))
+    late = sum_everywhere((grad_kern, grad_cbias))
+    reduced = late + early
+    owned_in, owned_out = (scatter_sum_rows(grad_inproj), scatter_sum_rows(grad_outproj))
     return (
         block_out.reshape(1, row_count, col_count, channels),
         grad_feat[None],

time: 585 us -> 261 us (0.45)
  waiting for transfers between devices: 397 us -> 47.7 us
  blocking collectives: 41 us -> 0 us
  starting transfers between devices: 11.4 us -> 48.4 us
  other arithmetic: 57.2 us -> 92.1 us
  local copies, waits for them, and re-layouts: 8.29 us -> 21.1 us
  between operations: 14.1 us -> 3.21 us
  matrix products: 54.5 us -> 44.9 us
    reduce_scatter x2 -> x0, waiting for transfers between devices: 292 us -> none  [the longest x1 148 us: local(): lax.psum_scatter(grad_outproj, ('dp', 'space'), scatter_dimension=0, tile...]
    all_gather x2 -> x0, waiting for transfers between devices: 61.2 us -> none  [the longest x1 35 us: local(): lax.all_gather(weight_out, ('dp', 'space'), axis=0, tiled=True)]
    ppermute x0 -> x30, waiting for transfers between devices: none -> 47.7 us  [swapped(): lax.ppermute(x, axis, [(i, i ^ stride) for i in range(lax.axis_size(axis))])]
    psum x1 -> x0, waiting for transfers between devices: 41.1 us -> none  [local(): lax.psum((grad_kern, grad_cbias, grad_gain, grad_normbias, grad_inbias, g...]
    psum x1 -> x0, blocking collectives: 41 us -> none  [local(): lax.psum((grad_kern, grad_cbias, grad_gain, grad_normbias, grad_inbias, g...]
    ppermute x0 -> x30, starting transfers between devices: none -> 35.1 us  [swapped(): lax.ppermute(x, axis, [(i, i ^ stride) for i in range(lax.axis_size(axis))])]
    convert_element_type x0 -> x1, other arithmetic: none -> 19.5 us  [norm_mlp(): hidden = hidden_wide.astype(jnp.bfloat16)]
    convert_element_type x0 -> x11, local copies, waits for them, and re-layouts: none -> 8.84 us  [the longest x1 6.47 us: norm_mlp(): hidden = hidden_wide.astype(jnp.bfloat16)]
  transfers between devices with their start and end apart: 9 -> 34, of which waited for: 6 -> 12; matrix products, arithmetic and copies ran while one was open for 14% -> 48% of each run, Pallas kernels for 0% -> 0%
where the time goes in v1:
time: 261 us; the launch traced here: 257 us
  other arithmetic  92.1 us (35%)
  starting transfers between devices  48.4 us (19%)
  waiting for transfers between devices  47.7 us (18%)
  matrix products  44.9 us (17%)
  local copies, waits for them, and re-layouts  21.1 us (8%)
  between operations  3.21 us (1%)
    ppermute x30, waiting for transfers between devices, swapped(): lax.ppermute(x, axis, [(i, i ^ stride) for i in range(lax.axis_size(axis))])  47.7 us
    ppermute x30, starting transfers between devices, swapped(): lax.ppermute(x, axis, [(i, i ^ stride) for i in range(lax.axis_size(axis))])  35.1 us
    convert_element_type x1, other arithmetic, norm_mlp(): hidden = hidden_wide.astype(jnp.bfloat16)  19.5 us
    dot_general x1, matrix products, norm_mlp(): jnp.dot(activated, weight_in, preferred_element_type=jnp.float32) + bias_in  19.1 us
    broadcast_in_dim x1, other arithmetic, local(): grad_feat[None]  17.9 us
    reduce_sum x1, other arithmetic, norm_mlp(): center = jnp.mean(widened, axis=-1, keepdims=True)  16.9 us
    reduce_sum x3, other arithmetic, kernel_gradient(): tap_line.append(jnp.sum(grad_wide * window, axis=(0, 1)))  16.1 us
    ppermute x2, starting transfers between devices, padded_2(): before = lax.ppermute(last, axis, up)  10.7 us
  transfers between devices with their start and end apart: 34, of which 12 were waited for; matrix products, arithmetic and copies ran while one was open for 48% of the time, Pallas kernels for 0%

profile of v1, /device:TPU:0, one launch (start us, length us, event | category | flops | bytes accessed | tf_op | source)
XLA Modules:
  0.0 257.4 jit_solution(15475811181528814189)
XLA Ops:
  3.2 5.5 %collective-permute-start = (bf16[32,3,512]{2,1,0:T(4,128)(2,1)S(1)}, bf16[32,3,512]{2,1,0:T(4,128)(2,1)S(1)}, u32[]{:S(2)}, u32[]{:S(2)}) collective-permute-start(bf16[32,3,512]{2,1,0:T(4,128)(2,1)S(1)} %get-tuple-element.92), channel_id=1, source_target_pairs={{0,1},{1,2},{2,3},{3,4},{4,5},{5,6},{6,7},{8,9},{9,10},{10,11},{11... | collective-permute-start | bytes 294920 | tf_op jit(solution)/shard_map/ppermute | solution.py:19
  8.7 3.1 %collective-permute-start.2 = (bf16[16,2048]{1,0:T(8,128)(2,1)}, bf16[16,2048]{1,0:T(8,128)(2,1)S(1)}, u32[]{:S(2)}, u32[]{:S(2)}) collective-permute-start(bf16[16,2048]{1,0:T(8,128)(2,1)} %param.17), channel_id=1, source_target_pairs={{0,4},{1,5},{2,6},{3,7},{4,0},{5,1},{6,2},{7,3},{8,12},{9,13},{10,... | collective-permute-start | bytes 196616 | tf_op jit(solution)/shard_map/ppermute | solution.py:41
  14.6 3.2 %multiply_reduce_fusion.3 = (f32[512]{0:T(512)}, bf16[1,32,32,512]{3,2,1,0:T(8,128)(2,1)}) fusion(bf16[1,32,32,512]{3,2,1,0:T(8,128)(2,1)} %param.12, f32[512]{0:T(512)} %param.21), kind=kLoop, calls=%fused_computation.293 | loop fusion | flops 2096640 | bytes 2101248 | tf_op jit(solution)/shard_map/reduce_sum | solution.py:155
  23.0 16.9 %convert_reduce_fusion.1 = (f32[32,32]{1,0:T(8,128)S(1)}, bf16[32,32,512]{2,1,0:T(8,128)(2,1)S(1)}) fusion(f32[512]{0:T(512)S(1)} %copy-done.95, bf16[38,38,512]{2,1,0:T(8,128)(2,1)S(1)} %select_maximum_fusion.2, f32[512]{0:T(512)} %bitcast.50, f32[512]{0:T(512)} %bitcast.49, f32[512]{0:T(512)S(1)} %bitcast.406, f32[512]{0:T(512)S(1)} %bitcast.408, ...), kind=kLoop, calls=%fused_computation.295 | loop fusion | flops 88079360 | bytes 46440448 | tf_op jit(solution)/shard_map/reduce_sum | solution.py:141
  40.0 2.7 %collective-permute-start.4 = (bf16[2,2,16,2048]{3,2,1,0:T(8,128)(2,1)S(1)}, bf16[2,2,16,2048]{3,2,1,0:T(8,128)(2,1)S(1)}, u32[]{:S(2)}, u32[]{:S(2)}) collective-permute-start(bf16[2,2,16,2048]{3,2,1,0:T(8,128)(2,1)S(1)} %pad_maximum_fusion.10), channel_id=1, source_target_pairs={{0,1},{1,0},{2,3},{3,2},{4,5},{5,4},{6,7},{7,6},{8,9},{9,8},{10,11... | collective-permute-start | bytes 786440 | tf_op jit(solution)/shard_map/ppermute | solution.py:41
  42.9 7.1 %collective-permute-done.4 = bf16[2,2,16,2048]{3,2,1,0:T(8,128)(2,1)S(1)} collective-permute-done((bf16[2,2,16,2048]{3,2,1,0:T(8,128)(2,1)S(1)}, bf16[2,2,16,2048]{3,2,1,0:T(8,128)(2,1)S(1)}, u32[]{:S(2)}, u32[]{:S(2)}) %collective-permute-start.4) | collective-permute-done | bytes 262176 | tf_op jit(solution)/shard_map/ppermute | solution.py:41
  55.5 9.0 %collective-permute-done.5 = bf16[2,2,2,16,2048]{4,3,2,1,0:T(8,128)(2,1)S(1)} collective-permute-done((bf16[2,2,2,16,2048]{4,3,2,1,0:T(8,128)(2,1)S(1)}, bf16[2,2,2,16,2048]{4,3,2,1,0:T(8,128)(2,1)S(1)}, u32[]{:S(2)}, u32[]{:S(2)}) %collective-permute-start.5) | collective-permute-done | bytes 524320 | tf_op jit(solution)/shard_map/ppermute | solution.py:41
  74.1 19.1 %fusion = (f32[1024,2048]{1,0:T(8,128)S(1)}, f32[1024,2048]{1,0:T(8,128)S(1)}) fusion(f32[2048]{0:T(1024)S(1)} %copy-done.14, bf16[1024,512]{1,0:T(8,128)(2,1)S(1)} %bitcast.398, bf16[512,2048]{1,0:T(8,128)(2,1)S(1)} %bitcast.393), kind=kOutput, calls=%fused_computation.51 | convolution fusion | flops 2279604224 | bytes 19931136 | tf_op jit(solution)/shard_map/dot_general | solution.py:146
  93.2 19.5 %fusion.3 = bf16[2048,1024]{0,1:T(8,128)(2,1)} fusion(f32[1024,2048]{1,0:T(8,128)S(1)} %get-tuple-element.162, f32[2048]{0:T(1024)S(1)} %copy-done.14), kind=kLoop, calls=%fused_computation.54 | loop fusion | flops 138412032 | bytes 12591104 | tf_op jit(solution)/shard_map/convert_element_type | solution.py:148
  114.0 6.7 %fusion.185 = (f32[2048]{0:T(1024)S(1)}, bf16[1024,2048]{1,0:T(8,128)(2,1)}) fusion(f32[1024,2048]{1,0:T(8,128)S(1)} %get-tuple-element.161, bf16[1024,512]{1,0:T(8,128)(2,1)S(1)} %bitcast.395, bf16[2048,512]{1,0:T(8,128)(2,1)S(1)} %bitcast.390, f32[1024,2048]{1,0:T(8,128)S(1)} %get-tuple-element.162, f32[2048]{0:T(1024)S(1)} %copy-done.14), kind=kOutput, calls=%fused_computation.405 | convolution fusion | flops 2181036032 | bytes 24133632 | tf_op jit(solution)/shard_map/dot_general | solution.py:159
  120.7 6.3 %multiply_reduce_fusion = (f32[512]{0:T(512)S(1)}, f32[1024]{0:T(1024)S(1)}, f32[1024]{0:T(1024)S(1)}, f32[512]{0:T(512)S(1)}, bf16[1024,512]{1,0:T(8,128)(2,1)}, /*index=5*/f32[1024,512]{1,0:T(8,128)S(1)}) fusion(bf16[32,32,512]{2,1,0:T(8,128)(2,1)S(1)} %copy-done.3, f32[1024]{0:T(1024)S(1)} %div.65, f32[1024]{0:T(1024)S(1)} %rsqrt.13, ...), kind=kOutput, calls=%fused_computation.284 | convolution fusion | flops 2154296320 | bytes 10510336 | tf_op jit(solution)/shard_map/dot_general | solution.py:168
  127.0 6.5 %fusion.151 = (f32[512]{0:T(512)S(1)}, f32[512]{0:T(512)S(1)}, f32[512]{0:T(512)S(1)}, f32[512]{0:T(512)S(1)}, f32[512]{0:T(512)S(1)}, /*index=5*/f32[512]{0:T(5...) fusion(bf16[38,38,512]{2,1,0:T(8,128)(2,1)S(1)} %select_maximum, ...), kind=kLoop, calls=%fused_computation.270 | loop fusion | flops 33545216 | bytes 23123968 | tf_op jit(solution)/shard_map/reduce_sum | solution.py:123
  133.5 5.2 %fusion.133 = (f32[512]{0:T(512)S(1)}, f32[512]{0:T(512)S(1)}, f32[512]{0:T(512)S(1)}, f32[512]{0:T(512)S(1)}, f32[512]{0:T(512)S(1)}, /*index=5*/f32[512]{0:T(5...) fusion(bf16[38,38,512]{2,1,0:T(8,128)(2,1)S(1)} %select_maximum, ...), kind=kLoop, calls=%fused_computation.252 | loop fusion | flops 28826624 | bytes 19959808 | tf_op jit(solution)/shard_map/reduce_sum | solution.py:123
  138.8 3.9 %fusion.152 = (f32[512]{0:T(512)S(1)}, bf16[1024,512]{1,0:T(8,128)(2,1)}, f32[512]{0:T(512)S(1)}, f32[512]{0:T(512)S(1)}) fusion(bf16[1,32,32,512]{3,2,1,0:T(8,128)(2,1)S(1)} %copy-done.4, f32[512]{0:T(512)S(1)} %copy-done.97, f32[512]{0:T(512)S(1)} %copy-done.94, bf16[1,32,32,512]{3,2,1,0:T(8,128)(2,1)S(1)} %copy-done.1, ...), kind=kOutput, calls=%fused_computation.276 | convolution fusion | flops 2162162176 | bytes 23087104 | tf_op jit(solution)/shard_map/dot_general | solution.py:149
  144.8 5.2 %collective-permute-start.12 = (bf16[32,3,512]{2,1,0:T(4,128)(2,1)}, bf16[32,3,512]{2,1,0:T(4,128)(2,1)}, u32[]{:S(2)}, u32[]{:S(2)}) collective-permute-start(bf16[32,3,512]{2,1,0:T(4,128)(2,1)} %get-tuple-element.88), channel_id=1, source_target_pairs={{0,1},{1,2},{2,3},{3,4},{4,5},{5,6},{6,7},{8,9},{9,10},{10,11},{11... | collective-permute-start | bytes 294920 | tf_op jit(solution)/shard_map/ppermute | solution.py:19
  150.0 4.4 %fusion.130 = (f32[512]{0:T(512)S(1)}, f32[512]{0:T(512)S(1)}, f32[512]{0:T(512)S(1)}, f32[512]{0:T(512)S(1)}, f32[512]{0:T(512)S(1)}, /*index=5*/f32[512]{0:T(5...) fusion(bf16[32,3,512]{2,1,0:T(4,128)(2,1)S(1)} %collective-perm, ...), kind=kLoop, calls=%fused_computation.249 | loop fusion | flops 28829696 | bytes 8609792 | tf_op jit(solution)/shard_map/reduce_sum | solution.py:123
  158.5 4.5 %fusion.24 = f32[2,2,2,2,2,16,2048]{6,5,4,3,2,1,0:T(8,128)S(1)} fusion(bf16[2,2,2,2,2,16,1024]{6,5,4,3,2,1,0:T(8,128)(2,1)S(1)} %bitcast.399, bf16[1024,2048]{1,0:T(8,128)(2,1)} %get-tuple-element.165), kind=kOutput, calls=%fused_computation.92 | convolution fusion | flops 2147483648 | bytes 9437184 | tf_op jit(solution)/shard_map/dot_general | solution.py:165
  165.6 6.5 %copy.31 = bf16[2048,1024]{1,0:T(8,128)(2,1)} copy(bf16[2048,1024]{0,1:T(8,128)(2,1)} %fusion.3) | data formatting | bytes 8388608 | tf_op jit(solution)/shard_map/convert_element_type | solution.py:148
  174.4 4.5 %fusion.186 = f32[2,2,2,2,2,64,512]{6,5,4,3,2,1,0:T(8,128)S(1)} fusion(bf16[2,2,2,2,2,64,1024]{6,5,4,3,2,1,0:T(8,128)(2,1)} %bitcast.392, bf16[1024,512,1,1,1,1,1]{1,0,6,5,4,3,2:T(8,128)(2,1)S(1)} %bitcast.396), kind=kOutput, calls=%fused_computation.406 | convolution fusion | flops 2147483648 | bytes 9437184 | tf_op jit(solution)/shard_map/dot_general | solution.py:156
  186.0 4.4 %collective-permute-done.15 = f32[50,512]{1,0:T(8,128)S(1)} collective-permute-done((f32[50,512]{1,0:T(8,128)S(1)}, f32[50,512]{1,0:T(8,128)S(1)}, u32[]{:S(2)}, u32[]{:S(2)}) %collective-permute-start.15) | collective-permute-done | bytes 102432 | tf_op jit(solution)/shard_map/ppermute | solution.py:41
  205.3 17.9 %fusion.169 = bf16[1,32,32,512]{3,2,1,0:T(8,128)(2,1)} fusion(bf16[38,38,512]{2,1,0:T(8,128)(2,1)S(1)} %select_maximum_fusion, f32[512]{0:T(512)} %bitcast.50, f32[512]{0:T(512)} %bitcast.49, f32[512]{0:T(512)S(1)} %bitcast.407, f32[512]{0:T(512)S(1)} %bitcast.409, f32[512]{0:T(512)S(1)} %bitcast.411, f32[512]{0:T(512)S(1)} %bitcast.413, ...), kind=kLoop, calls=%fused_computation.342 | loop fusion | flops 87556096 | bytes 47482880 | tf_op jit(solution)/shard_map/broadcast_in_dim | solution.py:246
  231.1 6.8 %collective-permute-done.30 = bf16[2,2,2,64,512]{4,3,2,1,0:T(8,128)(2,1)S(1)} collective-permute-done((bf16[2,2,2,64,512]{4,3,2,1,0:T(8,128)(2,1)S(1)}, bf16[2,2,2,64,512]{4,3,2,1,0:T(8,128)(2,1)S(1)}, u32[]{:S(2)}, u32[]{:S(2)}) %collective-permute-start.30) | collective-permute-done | bytes 524320 | tf_op jit(solution)/shard_map/ppermute | solution.py:41
  241.5 3.1 %collective-permute-done.31 = bf16[2,2,64,512]{3,2,1,0:T(8,128)(2,1)S(1)} collective-permute-done((bf16[2,2,64,512]{3,2,1,0:T(8,128)(2,1)S(1)}, bf16[2,2,64,512]{3,2,1,0:T(8,128)(2,1)S(1)}, u32[]{:S(2)}, u32[]{:S(2)}) %collective-permute-start.31) | collective-permute-done | bytes 262176 | tf_op jit(solution)/shard_map/ppermute | solution.py:41
  252.9 3.5 %collective-permute-done.33 = bf16[64,512]{1,0:T(8,128)(2,1)S(1)} collective-permute-done((bf16[64,512]{1,0:T(8,128)(2,1)S(1)}, bf16[64,512]{1,0:T(8,128)(2,1)S(1)}, u32[]{:S(2)}, u32[]{:S(2)}) %collective-permute-start.33) | collective-permute-done | bytes 65568 | tf_op jit(solution)/shard_map/ppermute | solution.py:41
  (342 shorter events, 78.8 us)
Async XLA Ops:
  1.9 19.9 %collective-permute-start.1 = (bf16[32,3,512]{2,1,0:T(4,128)(2,1)S(1)}, bf16[32,3,512]{2,1,0:T(4,128)(2,1)S(1)}, u32[]{:S(2)}, u32[]{:S(2)}) collective-permute-start(bf16[32,3,512]{2,1,0:T(4,128)(2,1)S(1)} %get-tuple-element.93), channel_id=1, source_target_pairs={{1,0},{2,1},{3,2},{4,3},{5,4},{6,5},{7,6},{9,8},{10,9},{11,10},{12... | collective-permute-start | bytes 294920 | tf_op jit(solution)/shard_map/ppermute | solution.py:20
  3.2 18.6 %collective-permute-start = (bf16[32,3,512]{2,1,0:T(4,128)(2,1)S(1)}, bf16[32,3,512]{2,1,0:T(4,128)(2,1)S(1)}, u32[]{:S(2)}, u32[]{:S(2)}) collective-permute-start(bf16[32,3,512]{2,1,0:T(4,128)(2,1)S(1)} %get-tuple-element.92), channel_id=1, source_target_pairs={{0,1},{1,2},{2,3},{3,4},{4,5},{5,6},{6,7},{8,9},{9,10},{10,11},{11... | collective-permute-start | bytes 294920 | tf_op jit(solution)/shard_map/ppermute | solution.py:19
  8.7 10.8 %collective-permute-start.2 = (bf16[16,2048]{1,0:T(8,128)(2,1)}, bf16[16,2048]{1,0:T(8,128)(2,1)S(1)}, u32[]{:S(2)}, u32[]{:S(2)}) collective-permute-start(bf16[16,2048]{1,0:T(8,128)(2,1)} %param.17), channel_id=1, source_target_pairs={{0,4},{1,5},{2,6},{3,7},{4,0},{5,1},{6,2},{7,3},{8,12},{9,13},{10,... | collective-permute-start | bytes 196616 | tf_op jit(solution)/shard_map/ppermute | solution.py:41
  11.9 9.7 %collective-permute-start.7 = (bf16[64,512]{1,0:T(8,128)(2,1)}, bf16[64,512]{1,0:T(8,128)(2,1)S(1)}, u32[]{:S(2)}, u32[]{:S(2)}) collective-permute-start(bf16[64,512]{1,0:T(8,128)(2,1)} %param.19), channel_id=1, source_target_pairs={{0,4},{1,5},{2,6},{3,7},{4,0},{5,1},{6,2},{7,3},{8,12},{9,13},{10,... | collective-permute-start | bytes 196616 | tf_op jit(solution)/shard_map/ppermute | solution.py:41
  19.6 20.3 %collective-permute-start.3 = (bf16[2,16,2048]{2,1,0:T(8,128)(2,1)S(1)}, bf16[2,16,2048]{2,1,0:T(8,128)(2,1)S(1)}, u32[]{:S(2)}, u32[]{:S(2)}) collective-permute-start(bf16[2,16,2048]{2,1,0:T(8,128)(2,1)S(1)} %pad_maximum_fusion.12), channel_id=1, source_target_pairs={{0,2},{1,3},{2,0},{3,1},{4,6},{5,7},{6,4},{7,5},{8,10},{9,11},{10,... | collective-permute-start | bytes 393224 | tf_op jit(solution)/shard_map/ppermute | solution.py:41
  21.6 21.2 %collective-permute-start.8 = (bf16[2,64,512]{2,1,0:T(8,128)(2,1)S(1)}, bf16[2,64,512]{2,1,0:T(8,128)(2,1)S(1)}, u32[]{:S(2)}, u32[]{:S(2)}) collective-permute-start(bf16[2,64,512]{2,1,0:T(8,128)(2,1)S(1)} %pad_maximum_fusion.13), channel_id=1, source_target_pairs={{0,2},{1,3},{2,0},{3,1},{4,6},{5,7},{6,4},{7,5},{8,10},{9,11},{10,... | collective-permute-start | bytes 393224 | tf_op jit(solution)/shard_map/ppermute | solution.py:41
  40.0 10.0 %collective-permute-start.4 = (bf16[2,2,16,2048]{3,2,1,0:T(8,128)(2,1)S(1)}, bf16[2,2,16,2048]{3,2,1,0:T(8,128)(2,1)S(1)}, u32[]{:S(2)}, u32[]{:S(2)}) collective-permute-start(bf16[2,2,16,2048]{3,2,1,0:T(8,128)(2,1)S(1)} %pad_maximum_fusion.10), channel_id=1, source_target_pairs={{0,1},{1,0},{2,3},{3,2},{4,5},{5,4},{6,7},{7,6},{8,9},{9,8},{10,11... | collective-permute-start | bytes 786440 | tf_op jit(solution)/shard_map/ppermute | solution.py:41
  42.8 10.2 %collective-permute-start.9 = (bf16[2,2,64,512]{3,2,1,0:T(8,128)(2,1)S(1)}, bf16[2,2,64,512]{3,2,1,0:T(8,128)(2,1)S(1)}, u32[]{:S(2)}, u32[]{:S(2)}) collective-permute-start(bf16[2,2,64,512]{3,2,1,0:T(8,128)(2,1)S(1)} %pad_maximum_fusion.11), channel_id=1, source_target_pairs={{0,1},{1,0},{2,3},{3,2},{4,5},{5,4},{6,7},{7,6},{8,9},{9,8},{10,11... | collective-permute-start | bytes 786440 | tf_op jit(solution)/shard_map/ppermute | solution.py:41
  50.1 14.4 %collective-permute-start.5 = (bf16[2,2,2,16,2048]{4,3,2,1,0:T(8,128)(2,1)S(1)}, bf16[2,2,2,16,2048]{4,3,2,1,0:T(8,128)(2,1)S(1)}, u32[]{:S(2)}, u32[]{:S(2)}) collective-permute-start(bf16[2,2,2,16,2048]{4,3,2,1,0:T(8,128)(2,1)S(1)} %pad_maximum_fusion.8), channel_id=1, source_target_pairs={{0,16},{8,24},{16,0},{24,8},{1,17},{9,25},{17,1},{25,9},{2,18},{10... | collective-permute-start | bytes 1572872 | tf_op jit(solution)/shard_map/ppermute | solution.py:41
  54.0 16.7 %collective-permute-start.10 = (bf16[2,2,2,64,512]{4,3,2,1,0:T(8,128)(2,1)}, bf16[2,2,2,64,512]{4,3,2,1,0:T(8,128)(2,1)}, u32[]{:S(2)}, u32[]{:S(2)}) collective-permute-start(bf16[2,2,2,64,512]{4,3,2,1,0:T(8,128)(2,1)} %pad_maximum_fusion.9), channel_id=1, source_target_pairs={{0,16},{8,24},{16,0},{24,8},{1,17},{9,25},{17,1},{25,9},{2,18},{10... | collective-permute-start | bytes 1572872 | tf_op jit(solution)/shard_map/ppermute | solution.py:41
  65.6 6.4 %collective-permute-start.6 = (bf16[2,2,2,2,16,2048]{5,4,3,2,1,0:T(8,128)(2,1)}, bf16[2,2,2,2,16,2048]{5,4,3,2,1,0:T(8,128)(2,1)}, u32[]{:S(2)}, u32[]{:S(2)}) collective-permute-start(bf16[2,2,2,2,16,2048]{5,4,3,2,1,0:T(8,128)(2,1)} %pad_maximum_fusion.6), channel_id=1, source_target_pairs={{0,8},{8,0},{16,24},{24,16},{1,9},{9,1},{17,25},{25,17},{2,10},{10... | collective-permute-start | bytes 3145736 | tf_op jit(solution)/shard_map/ppermute | solution.py:41
  71.9 40.7 %collective-permute-start.11 = (bf16[2,2,2,2,64,512]{5,4,3,2,1,0:T(8,128)(2,1)S(1)}, bf16[2,2,2,2,64,512]{5,4,3,2,1,0:T(8,128)(2,1)S(1)}, u32[]{:S(2)}, u32[]{:S(2)}) collective-permute-start(bf16[2,2,2,2,64,512]{5,4,3,2,1,0:T(8,128)(2,1)S(1)} %pad_maximum_fusion.7), channel_id=1, source_target_pairs={{0,8},{8,0},{16,24},{24,16},{1,9},{9,1},{17,25},{25,17},{2,10},{10... | collective-permute-start | bytes 3145736 | tf_op jit(solution)/shard_map/ppermute | solution.py:41
  143.5 52.4 %collective-permute-start.13 = (bf16[32,3,512]{2,1,0:T(4,128)(2,1)}, bf16[32,3,512]{2,1,0:T(4,128)(2,1)S(1)}, u32[]{:S(2)}, u32[]{:S(2)}) collective-permute-start(bf16[32,3,512]{2,1,0:T(4,128)(2,1)} %get-tuple-element.89), channel_id=1, source_target_pairs={{1,0},{2,1},{3,2},{4,3},{5,4},{6,5},{7,6},{9,8},{10,9},{11,10},{12... | collective-permute-start | bytes 294920 | tf_op jit(solution)/shard_map/ppermute | solution.py:20
  144.8 51.1 %collective-permute-start.12 = (bf16[32,3,512]{2,1,0:T(4,128)(2,1)}, bf16[32,3,512]{2,1,0:T(4,128)(2,1)}, u32[]{:S(2)}, u32[]{:S(2)}) collective-permute-start(bf16[32,3,512]{2,1,0:T(4,128)(2,1)} %get-tuple-element.88), channel_id=1, source_target_pairs={{0,1},{1,2},{2,3},{3,4},{4,5},{5,6},{6,7},{8,9},{9,10},{10,11},{11... | collective-permute-start | bytes 294920 | tf_op jit(solution)/shard_map/ppermute | solution.py:19
  155.0 28.7 %collective-permute-start.14 = (f32[50,512]{1,0:T(8,128)S(1)}, f32[50,512]{1,0:T(8,128)}, u32[]{:S(2)}, u32[]{:S(2)}) collective-permute-start(f32[50,512]{1,0:T(8,128)S(1)} %pad_maximum_fusion.14), channel_id=1, source_target_pairs={{0,8},{8,0},{16,24},{24,16},{1,9},{9,1},{17,25},{25,17},{2,10},{10... | collective-permute-start | bytes 307208 | tf_op jit(solution)/shard_map/ppermute | solution.py:41
  163.1 9.1 %collective-permute-start.21 = (f32[8,512]{1,0:T(8,128)S(1)}, f32[8,512]{1,0:T(8,128)}, u32[]{:S(2)}, u32[]{:S(2)}) collective-permute-start(f32[8,512]{1,0:T(8,128)S(1)} %add.620), channel_id=1, source_target_pairs={{0,1},{1,0},{2,3},{3,2},{4,5},{5,4},{6,7},{7,6},{8,9},{9,8},{10,11... | collective-permute-start | bytes 49160 | tf_op jit(solution)/shard_map/ppermute | solution.py:41
  165.6 36.5 %collective-permute-start.24 = (bf16[2,2,2,2,16,2048]{5,4,3,2,1,0:T(8,128)(2,1)S(1)}, bf16[2,2,2,2,16,2048]{5,4,3,2,1,0:T(8,128)(2,1)}, u32[]{:S(2)}, u32[]{:S(2)}) collective-permute-start(bf16[2,2,2,2,16,2048]{5,4,3,2,1,0:T(8,128)(2,1)S(1)} %fusion.167), channel_id=1, source_target_pairs={{0,8},{8,0},{16,24},{24,16},{1,9},{9,1},{17,25},{25,17},{2,10},{10... | collective-permute-start | bytes 3145736 | tf_op jit(solution)/shard_map/ppermute | solution.py:41
  183.7 40.7 %collective-permute-start.29 = (bf16[2,2,2,2,64,512]{5,4,3,2,1,0:T(8,128)(2,1)}, bf16[2,2,2,2,64,512]{5,4,3,2,1,0:T(8,128)(2,1)}, u32[]{:S(2)}, u32[]{:S(2)}) collective-permute-start(bf16[2,2,2,2,64,512]{5,4,3,2,1,0:T(8,128)(2,1)} %fusion.168), channel_id=1, source_target_pairs={{0,8},{8,0},{16,24},{24,16},{1,9},{9,1},{17,25},{25,17},{2,10},{10... | collective-permute-start | bytes 3145736 | tf_op jit(solution)/shard_map/ppermute | solution.py:41
  200.7 22.5 %collective-permute-start.18 = (f32[50,512]{1,0:T(8,128)S(1)}, f32[50,512]{1,0:T(8,128)S(1)}, u32[]{:S(2)}, u32[]{:S(2)}) collective-permute-start(f32[50,512]{1,0:T(8,128)S(1)} %add.617), channel_id=1, source_target_pairs={{0,4},{1,5},{2,6},{3,7},{4,0},{5,1},{6,2},{7,3},{8,12},{9,13},{10,... | collective-permute-start | bytes 307208 | tf_op jit(solution)/shard_map/ppermute | solution.py:41
  204.4 23.9 %collective-permute-start.25 = (bf16[2,2,2,16,2048]{4,3,2,1,0:T(8,128)(2,1)}, bf16[2,2,2,16,2048]{4,3,2,1,0:T(8,128)(2,1)}, u32[]{:S(2)}, u32[]{:S(2)}) collective-permute-start(bf16[2,2,2,16,2048]{4,3,2,1,0:T(8,128)(2,1)} %fusion.170), channel_id=1, source_target_pairs={{0,16},{8,24},{16,0},{24,8},{1,17},{9,25},{17,1},{25,9},{2,18},{10... | collective-permute-start | bytes 1572872 | tf_op jit(solution)/shard_map/ppermute | solution.py:41
  226.8 11.1 %collective-permute-start.30 = (bf16[2,2,2,64,512]{4,3,2,1,0:T(8,128)(2,1)S(1)}, bf16[2,2,2,64,512]{4,3,2,1,0:T(8,128)(2,1)S(1)}, u32[]{:S(2)}, u32[]{:S(2)}) collective-permute-start(bf16[2,2,2,64,512]{4,3,2,1,0:T(8,128)(2,1)S(1)} %fusion.171), channel_id=1, source_target_pairs={{0,16},{8,24},{16,0},{24,8},{1,17},{9,25},{17,1},{25,9},{2,18},{10... | collective-permute-start | bytes 1572872 | tf_op jit(solution)/shard_map/ppermute | solution.py:41
  229.6 10.0 %collective-permute-start.26 = (bf16[2,2,16,2048]{3,2,1,0:T(8,128)(2,1)S(1)}, bf16[2,2,16,2048]{3,2,1,0:T(8,128)(2,1)S(1)}, u32[]{:S(2)}, u32[]{:S(2)}) collective-permute-start(bf16[2,2,16,2048]{3,2,1,0:T(8,128)(2,1)S(1)} %fusion.172), channel_id=1, source_target_pairs={{0,1},{1,0},{2,3},{3,2},{4,5},{5,4},{6,7},{7,6},{8,9},{9,8},{10,11... | collective-permute-start | bytes 786440 | tf_op jit(solution)/shard_map/ppermute | solution.py:41
  238.1 6.4 %collective-permute-start.31 = (bf16[2,2,64,512]{3,2,1,0:T(8,128)(2,1)S(1)}, bf16[2,2,64,512]{3,2,1,0:T(8,128)(2,1)S(1)}, u32[]{:S(2)}, u32[]{:S(2)}) collective-permute-start(bf16[2,2,64,512]{3,2,1,0:T(8,128)(2,1)S(1)} %fusion.173), channel_id=1, source_target_pairs={{0,1},{1,0},{2,3},{3,2},{4,5},{5,4},{6,7},{7,6},{8,9},{9,8},{10,11... | collective-permute-start | bytes 786440 | tf_op jit(solution)/shard_map/ppermute | solution.py:41
  239.7 6.8 %collective-permute-start.27 = (bf16[2,16,2048]{2,1,0:T(8,128)(2,1)S(1)}, bf16[2,16,2048]{2,1,0:T(8,128)(2,1)S(1)}, u32[]{:S(2)}, u32[]{:S(2)}) collective-permute-start(bf16[2,16,2048]{2,1,0:T(8,128)(2,1)S(1)} %fusion.174), channel_id=1, source_target_pairs={{0,2},{1,3},{2,0},{3,1},{4,6},{5,7},{6,4},{7,5},{8,10},{9,11},{10,... | collective-permute-start | bytes 393224 | tf_op jit(solution)/shard_map/ppermute | solution.py:41
  (108 other events, 733.7 us)

commit v2 on v1

--- a/solution.py
+++ b/solution.py
@@ -1,6 +1,8 @@
 import jax
 import jax.numpy as jnp
 from jax import lax
+from jax.experimental import pallas as pl
+from jax.experimental.pallas import tpu as pltpu
 from jax.sharding import PartitionSpec as P
 
 KS = 7
@@ -22,13 +24,15 @@
     return x
 
 
-def index_bits():
+def index_bits(other_order=False):
     listed = []
     for axis in ("dp", "space"):
         stride = 1
         while stride < lax.axis_size(axis):
             listed.append((axis, stride))
             stride *= 2
+    if other_order:
+        listed[1], listed[2] = listed[2], listed[1]
     return listed
 
 
@@ -45,10 +49,10 @@
     return (lax.axis_index(key[0]) // key[1]) % 2
 
 
-def gather_rows(x):
+def gather_rows(x, other_order=False):
     tail = x.shape[1]
     present = []
-    for key in index_bits()[::-1]:
+    for key in index_bits(other_order)[::-1]:
         other = swapped(x, key)
         present = sorted(present + [key], key=row_order)
         at = present.index(key)
@@ -57,8 +61,8 @@
     return x.reshape(-1, tail)
 
 
-def scatter_sum_rows(x):
-    keys = index_bits()
+def scatter_sum_rows(x, other_order=False):
+    keys = index_bits(other_order)
     present = sorted(keys, key=row_order)
     x = x.reshape((2,) * len(keys) + (-1, x.shape[1]))
     for key in keys:
@@ -66,7 +70,7 @@
         bit = own_bit(key)
         kept = lax.dynamic_index_in_dim(x, bit, at, keepdims=False)
         sent = lax.dynamic_index_in_dim(x, 1 - bit, at, keepdims=False).astype(jnp.bfloat16)
-        x = kept + swapped(sent, key).astype(jnp.float32)
+        x = kept.astype(jnp.float32) + swapped(sent, key).astype(jnp.float32)
         present.remove(key)
     return x
 
@@ -81,10 +85,6 @@
         outs.append(flat[at : at + rows].reshape(part.shape))
         at += rows
     return outs
-
-
-def gelu_exact(inputs):
-    return jax.nn.gelu(inputs, approximate=False)
 
 
 def conv_forward(padded, kernel, offset, row_count, col_count):
@@ -125,6 +125,92 @@
     return jnp.stack(taps)
 
 
+def dot(a, b, over_a, over_b):
+    return lax.dot_general(
+        a, b, (((over_a,), (over_b,)), ((), ())), preferred_element_type=jnp.float32
+    )
+
+
+def norm_mlp_kernel(
+    conv_ref,
+    source_ref,
+    upstream_ref,
+    gain_ref,
+    bias_ref,
+    win_ref,
+    bin_ref,
+    wout_ref,
+    bout_ref,
+    scale_ref,
+    block_ref,
+    gconv_ref,
+    ggain_ref,
+    gnbias_ref,
+    gin_ref,
+    ginbias_ref,
+    gout_ref,
+    goutbias_ref,
+    gscale_ref,
+    gcbias_ref,
+    normed,
+    inv_std,
+    act,
+    dbranch,
+    branch,
+    dact,
+):
+    step = pl.program_id(0)
+
+    @pl.when(step == 0)
+    def _():
+        wide = conv_ref[...].astype(jnp.float32)
+        shifted = wide - jnp.mean(wide, axis=-1, keepdims=True)
+        inv = lax.rsqrt(jnp.mean(shifted * shifted, axis=-1, keepdims=True) + NORM_EPS)
+        inv_std[...] = inv
+        unit = shifted * inv
+        normed[...] = unit
+        act[...] = (unit * gain_ref[...] + bias_ref[...]).astype(jnp.bfloat16)
+        d_branch = scale_ref[...] * upstream_ref[...].astype(jnp.float32)
+        goutbias_ref[...] = jnp.sum(d_branch, axis=0, keepdims=True)
+        dbranch[...] = d_branch.astype(jnp.bfloat16)
+        branch[...] = jnp.zeros_like(branch)
+        dact[...] = jnp.zeros_like(dact)
+
+    pre = dot(act[...], win_ref[...], 1, 0) + bin_ref[...]
+    d_hidden = dot(dbranch[...], wout_ref[...], 1, 1)
+    cdf = 0.5 + 0.5 * lax.erf(pre * 0.7071067811865476)
+    slope = cdf + pre * (jnp.exp(pre * pre * -0.5) * 0.3989422804014327)
+    hidden = (pre * cdf).astype(jnp.bfloat16)
+    d_pre = d_hidden * slope
+    ginbias_ref[...] = jnp.sum(d_pre, axis=0, keepdims=True)
+    d_pre_b = d_pre.astype(jnp.bfloat16)
+    branch[...] += dot(hidden, wout_ref[...], 1, 0)
+    gout_ref[...] = dot(hidden, dbranch[...], 0, 0).astype(jnp.bfloat16)
+    dact[...] += dot(d_pre_b, win_ref[...], 1, 1)
+    gin_ref[...] = dot(act[...], d_pre_b, 0, 0).astype(jnp.bfloat16)
+
+    @pl.when(step == pl.num_programs(0) - 1)
+    def _():
+        full = branch[...] + bout_ref[...]
+        block_ref[...] = (source_ref[...].astype(jnp.float32) + scale_ref[...] * full).astype(
+            jnp.bfloat16
+        )
+        gscale_ref[...] = jnp.sum(upstream_ref[...].astype(jnp.float32) * full, 0, keepdims=True)
+        d_act = dact[...]
+        unit = normed[...]
+        ggain_ref[...] = jnp.sum(d_act * unit, axis=0, keepdims=True)
+        gnbias_ref[...] = jnp.sum(d_act, axis=0, keepdims=True)
+        scaled = d_act * gain_ref[...]
+        grad = inv_std[...] * (
+            scaled
+            - jnp.mean(scaled, axis=-1, keepdims=True)
+            - unit * jnp.mean(scaled * unit, axis=-1, keepdims=True)
+        )
+        grad_b = grad.astype(jnp.bfloat16)
+        gconv_ref[...] = grad_b
+        gcbias_ref[...] = jnp.sum(grad_b.astype(jnp.float32), axis=0, keepdims=True)
+
+
 def norm_mlp(
     conv_out,
     source,
@@ -137,57 +223,58 @@
     bias_out,
     layer_scale,
 ):
-    widened = conv_out.astype(jnp.float32)
-    center = jnp.mean(widened, axis=-1, keepdims=True)
-    shifted = widened - center
-    inv_std = lax.rsqrt(jnp.mean(shifted * shifted, axis=-1, keepdims=True) + NORM_EPS)
-    normed = shifted * inv_std
-    activated = (normed * norm_gain + norm_bias).astype(jnp.bfloat16)
-    pre_act = jnp.dot(activated, weight_in, preferred_element_type=jnp.float32) + bias_in
-    hidden_wide, gelu_back = jax.vjp(gelu_exact, pre_act)
-    hidden = hidden_wide.astype(jnp.bfloat16)
-    branch = jnp.dot(hidden, weight_out, preferred_element_type=jnp.float32) + bias_out
-    block_out = (source.astype(jnp.float32) + layer_scale * branch).astype(jnp.bfloat16)
-    upstream_wide = upstream.astype(jnp.float32)
-    d_branch = layer_scale * upstream_wide
-    d_branch_b = d_branch.astype(jnp.bfloat16)
-    grad_scale = jnp.sum(upstream_wide * branch, axis=0)
-    grad_outbias = jnp.sum(d_branch, axis=0)
-    grad_outproj = lax.dot_general(
-        hidden, d_branch_b, (((0,), (0,)), ((), ())), preferred_element_type=jnp.float32
-    )
-    d_hidden = lax.dot_general(
-        d_branch_b, weight_out, (((1,), (1,)), ((), ())), preferred_element_type=jnp.float32
-    )
-    d_pre = gelu_back(d_hidden)[0]
-    d_pre_b = d_pre.astype(jnp.bfloat16)
-    grad_inbias = jnp.sum(d_pre, axis=0)
-    grad_inproj = lax.dot_general(
-        activated, d_pre_b, (((0,), (0,)), ((), ())), preferred_element_type=jnp.float32
-    )
-    d_act = lax.dot_general(
-        d_pre_b, weight_in, (((1,), (1,)), ((), ())), preferred_element_type=jnp.float32
-    )
-    grad_gain = jnp.sum(d_act * normed, axis=0)
-    grad_normbias = jnp.sum(d_act, axis=0)
-    scaled = d_act * norm_gain
-    grad_conv = inv_std * (
-        scaled
-        - jnp.mean(scaled, axis=-1, keepdims=True)
-        - normed * jnp.mean(scaled * normed, axis=-1, keepdims=True)
-    )
-    return (
-        block_out,
-        grad_conv.astype(jnp.bfloat16),
-        (
-            grad_gain,
-            grad_normbias,
-            grad_inproj,
-            grad_inbias,
-            grad_outproj,
-            grad_outbias,
-            grad_scale,
+    pixels, channels = conv_out.shape
+    units = weight_in.shape[1]
+    tile = 256
+    whole = pl.BlockSpec((pixels, channels), lambda i: (0, 0))
+    row = pl.BlockSpec((1, channels), lambda i: (0, 0))
+    columns = pl.BlockSpec((channels, tile), lambda i: (0, i))
+    rows = pl.BlockSpec((tile, channels), lambda i: (i, 0))
+    unit_row = pl.BlockSpec((1, tile), lambda i: (0, i))
+    f32, bf16 = jnp.float32, jnp.bfloat16
+    shape = jax.ShapeDtypeStruct
+    vector = shape((1, channels), f32)
+    flops = 12 * pixels * channels * units
+    return pl.pallas_call(
+        norm_mlp_kernel,
+        grid=(units // tile,),
+        in_specs=[whole, whole, whole, row, row, columns, unit_row, rows, row, row],
+        out_specs=[whole, whole, row, row, columns, unit_row, rows, row, row, row],
+        out_shape=[
+            shape((pixels, channels), bf16),
+            shape((pixels, channels), bf16),
+            vector,
+            vector,
+            shape((channels, units), bf16),
+            shape((1, units), f32),
+            shape((units, channels), bf16),
+            vector,
+            vector,
+            vector,
+        ],
+        scratch_shapes=[
+            pltpu.VMEM((pixels, channels), f32),
+            pltpu.VMEM((pixels, 1), f32),
+            pltpu.VMEM((pixels, channels), bf16),
+            pltpu.VMEM((pixels, channels), bf16),
+            pltpu.VMEM((pixels, channels), f32),
+            pltpu.VMEM((pixels, channels), f32),
+        ],
+        compiler_params=pltpu.CompilerParams(vmem_limit_bytes=48 * 1024 * 1024),
+        cost_estimate=pl.CostEstimate(
+            flops=flops, bytes_accessed=16 * 1024 * 1024, transcendentals=pixels * units
         ),
+    )(
+        conv_out,
+        source,
+        upstream,
+        norm_gain[None],
+        norm_bias[None],
+        weight_in,
+        bias_in[None],
+        weight_out,
+        bias_out[None],
+        layer_scale[None],
     )
 
 
@@ -210,12 +297,12 @@
     row_count, col_count, channels = source.shape
     full_in, full_out = (
         gather_rows(weight_in),
-        gather_rows(weight_out),
+        gather_rows(weight_out, True),
     )
     rimmed = padded_2(source, (("space", 1),), reach)
     padded = jnp.pad(rimmed, ((reach, reach), (0, 0), (0, 0)))
     conv_out = conv_forward(padded, conv_kernel, conv_bias, row_count, col_count)
-    block_out, grad_conv, partials = norm_mlp(
+    block_out, grad_conv, *partials = norm_mlp(
         conv_out.reshape(-1, channels),
         source.reshape(-1, channels),
         upstream.reshape(-1, channels),
@@ -232,27 +319,33 @@
     grad_padded = jnp.pad(grad_rimmed, ((reach, reach), (0, 0), (0, 0)))
     conv_back = conv_backward(grad_padded, conv_kernel, row_count, col_count)
     grad_kern = kernel_gradient(grad_conv, padded, row_count, col_count)
-    grad_cbias = jnp.sum(grad_conv.astype(jnp.float32), axis=(0, 1))
     grad_feat = (upstream.astype(jnp.float32) + conv_back).astype(jnp.bfloat16)
-    grad_gain, grad_normbias, grad_inproj, grad_inbias, grad_outproj, grad_outbias, grad_scale = (
-        partials
-    )
-    early = sum_everywhere((grad_gain, grad_normbias, grad_inbias, grad_outbias, grad_scale))
-    late = sum_everywhere((grad_kern, grad_cbias))
-    reduced = late + early
-    owned_in, owned_out = (scatter_sum_rows(grad_inproj), scatter_sum_rows(grad_outproj))
+    (
+        grad_gain,
+        grad_normbias,
+        grad_inproj,
+        grad_inbias,
+        grad_outproj,
+        grad_outbias,
+        grad_scale,
+        grad_cbias,
+    ) = partials
+    reduced = sum_everywhere(
+        (grad_kern, grad_cbias, grad_gain, grad_normbias, grad_inbias, grad_outbias, grad_scale)
+    )
+    owned_in, owned_out = (scatter_sum_rows(grad_inproj), scatter_sum_rows(grad_outproj, True))
     return (
         block_out.reshape(1, row_count, col_count, channels),
         grad_feat[None],
         reduced[0],
-        reduced[1],
-        reduced[2],
-        reduced[3],
+        reduced[1].reshape(-1),
+        reduced[2].reshape(-1),
+        reduced[3].reshape(-1),
         owned_in,
-        reduced[4],
+        reduced[4].reshape(-1),
         owned_out,
-        reduced[5],
-        reduced[6],
+        reduced[5].reshape(-1),
+        reduced[6].reshape(-1),
     )
 
 

time: 261 us -> 185 us (0.71)
  matrix products: 44.9 us -> 0 us
  other arithmetic: 92.1 us -> 58.2 us
  Pallas kernels: 0 us -> 21.2 us
  starting transfers between devices: 48.4 us -> 40.6 us
  local copies, waits for them, and re-layouts: 21.1 us -> 15.6 us
    dot_general x6 -> x0, matrix products: 44.9 us -> none  [the longest x1 19.1 us: norm_mlp(): jnp.dot(activated, weight_in, preferred_element_type=jnp.float32) + bias_in]
    pallas_call x0 -> x1, Pallas kernels: none -> 21.2 us  [norm_mlp(): pl.pallas_call(norm_mlp_kernel, grid=(units // tile,), in_specs=[whole, w...]
    reduce_sum x3 -> x0, other arithmetic: 20.7 us -> none  [the longest x1 16.9 us: norm_mlp(): center = jnp.mean(widened, axis=-1, keepdims=True)]
    convert_element_type x1 -> x0, local copies, waits for them, and re-layouts: 6.47 us -> none  [norm_mlp(): hidden = hidden_wide.astype(jnp.bfloat16)]
    convert_element_type x2 -> x1, other arithmetic: 21.1 us -> 16.1 us  [conv_forward(): return (summed + offset).astype(jnp.bfloat16)]
    dynamic_slice x0 -> x4, local copies, waits for them, and re-layouts: none -> 5.03 us  [the longest x2 2.9 us: scatter_sum_rows(): kept = lax.dynamic_index_in_dim(x, bit, at, keepdims=False)]
    ppermute x2, starting transfers between devices: 10.7 us -> 6.63 us  [padded_2(): before = lax.ppermute(last, axis, up)]
    ppermute x30 -> x25, starting transfers between devices: 35.1 us -> 31.4 us  [swapped(): lax.ppermute(x, axis, [(i, i ^ stride) for i in range(lax.axis_size(axis))])]
  transfers between devices with their start and end apart: 34 -> 29, of which waited for: 12 -> 16; matrix products, arithmetic and copies ran while one was open for 48% -> 30% of each run, Pallas kernels for 0% -> 0%
where the time goes in v2:
time: 185 us; the launch traced here: 184 us
  other arithmetic  58.2 us (31%)
  waiting for transfers between devices  47 us (25%)
  starting transfers between devices  40.6 us (22%)
  Pallas kernels  21.2 us (11%)
  local copies, waits for them, and re-layouts  15.6 us (8%)
    ppermute x25, waiting for transfers between devices, swapped(): lax.ppermute(x, axis, [(i, i ^ stride) for i in range(lax.axis_size(axis))])  46.9 us
    ppermute x25, starting transfers between devices, swapped(): lax.ppermute(x, axis, [(i, i ^ stride) for i in range(lax.axis_size(axis))])  31.4 us
    pallas_call x1, Pallas kernels, norm_mlp(): pl.pallas_call(norm_mlp_kernel, grid=(units // tile,), in_specs=[whole, w...  21.2 us
    broadcast_in_dim x1, other arithmetic, local(): grad_feat[None]  16.6 us
    convert_element_type x1, other arithmetic, conv_forward(): return (summed + offset).astype(jnp.bfloat16)  16.1 us
    reduce_sum x4, other arithmetic, kernel_gradient(): tap_line.append(jnp.sum(grad_wide * window, axis=(0, 1)))  15.2 us
    ppermute x2, starting transfers between devices, padded_2(): before = lax.ppermute(last, axis, up)  6.63 us
    add x10, other arithmetic, scatter_sum_rows(): x = kept.astype(jnp.float32) + swapped(sent, key).astype(jnp.float32)  5.02 us
  transfers between devices with their start and end apart: 29, of which 16 were waited for; matrix products, arithmetic and copies ran while one was open for 30% of the time, Pallas kernels for 0%

profile of v2, /device:TPU:0, one launch (start us, length us, event | category | flops | bytes accessed | tf_op | source)
XLA Modules:
  0.0 184.0 jit_solution(7394190794875650368)
XLA Ops:
  0.6 4.1 %collective-permute-start.7 = (bf16[64,512]{1,0:T(8,128)(2,1)}, bf16[64,512]{1,0:T(8,128)(2,1)S(1)}, u32[]{:S(2)}, u32[]{:S(2)}) collective-permute-start(bf16[64,512]{1,0:T(8,128)(2,1)} %param.19), channel_id=1, source_target_pairs={{0,4},{1,5},{2,6},{3,7},{4,0},{5,1},{6,2},{7,3},{8,12},{9,13},{10,... | collective-permute-start | bytes 196616 | tf_op jit(solution)/shard_map/ppermute | solution.py:45
  6.0 3.7 %collective-permute-start = (bf16[32,3,512]{2,1,0:T(4,128)(2,1)S(1)}, bf16[32,3,512]{2,1,0:T(4,128)(2,1)S(1)}, u32[]{:S(2)}, u32[]{:S(2)}) collective-permute-start(bf16[32,3,512]{2,1,0:T(4,128)(2,1)S(1)} %get-tuple-element.102), channel_id=1, source_target_pairs={{0,1},{1,2},{2,3},{3,4},{4,5},{5,6},{6,7},{8,9},{9,10},{10,11},{11... | collective-permute-start | bytes 294920 | tf_op jit(solution)/shard_map/ppermute | solution.py:21
  15.2 3.7 %collective-permute-start.8 = (bf16[2,64,512]{2,1,0:T(8,128)(2,1)S(1)}, bf16[2,64,512]{2,1,0:T(8,128)(2,1)S(1)}, u32[]{:S(2)}, u32[]{:S(2)}) collective-permute-start(bf16[2,64,512]{2,1,0:T(8,128)(2,1)S(1)} %pad_maximum_fusion.13), channel_id=1, source_target_pairs={{0,2},{1,3},{2,0},{3,1},{4,6},{5,7},{6,4},{7,5},{8,10},{9,11},{10,... | collective-permute-start | bytes 393224 | tf_op jit(solution)/shard_map/ppermute | solution.py:45
  19.9 3.0 %collective-permute-done.8 = bf16[2,64,512]{2,1,0:T(8,128)(2,1)S(1)} collective-permute-done((bf16[2,64,512]{2,1,0:T(8,128)(2,1)S(1)}, bf16[2,64,512]{2,1,0:T(8,128)(2,1)S(1)}, u32[]{:S(2)}, u32[]{:S(2)}) %collective-permute-start.8) | collective-permute-done | bytes 131104 | tf_op jit(solution)/shard_map/ppermute | solution.py:45
  26.1 3.3 %collective-permute-done.9 = bf16[2,2,64,512]{3,2,0,1:T(8,128)(2,1)S(1)} collective-permute-done((bf16[2,2,64,512]{3,2,0,1:T(8,128)(2,1)S(1)}, bf16[2,2,64,512]{3,2,0,1:T(8,128)(2,1)S(1)}, u32[]{:S(2)}, u32[]{:S(2)}) %collective-permute-start.9) | collective-permute-done | bytes 262176 | tf_op jit(solution)/shard_map/ppermute | solution.py:45
  31.0 3.2 %collective-permute-done.4 = bf16[2,2,16,2048]{3,2,0,1:T(8,128)(2,1)S(1)} collective-permute-done((bf16[2,2,16,2048]{3,2,0,1:T(8,128)(2,1)S(1)}, bf16[2,2,16,2048]{3,2,0,1:T(8,128)(2,1)S(1)}, u32[]{:S(2)}, u32[]{:S(2)}) %collective-permute-start.4) | collective-permute-done | bytes 262176 | tf_op jit(solution)/shard_map/ppermute | solution.py:45
  36.7 6.0 %collective-permute-done.10 = bf16[2,2,2,64,512]{4,3,1,2,0:T(8,128)(2,1)S(1)} collective-permute-done((bf16[2,2,2,64,512]{4,3,1,2,0:T(8,128)(2,1)S(1)}, bf16[2,2,2,64,512]{4,3,1,2,0:T(8,128)(2,1)S(1)}, u32[]{:S(2)}, u32[]{:S(2)}) %collective-permute-start.10) | collective-permute-done | bytes 524320 | tf_op jit(solution)/shard_map/ppermute | solution.py:45
  43.8 16.1 %add_convert_fusion = bf16[32,32,512]{2,1,0:T(8,128)(2,1)S(1)} fusion(bf16[32,32,512]{2,1,0:T(8,128)(2,1)S(1)} %bitcast.284, bf16[32,3,512]{2,1,0:T(4,128)(2,1)S(1)} %collective-permute-done.1, bf16[32,3,512]{2,1,0:T(4,128)(2,1)S(1)} %collective-permute-done, f32[512]{0:T(512)S(1)} %copy-done.9, f32[512]{0:T(512)S(1)} %bitcast.392, f32[512]{0:T(512)S(1)} %bitcast.394, ...), kind=kLoop, calls=%fused_computation.228 | loop fusion | flops 87031808 | bytes 46436352 | tf_op jit(solution)/shard_map/convert_element_type | solution.py:98
  63.7 21.2 %shard_map.194 = (bf16[1024,512]{1,0:T(8,128)(2,1)}, bf16[1024,512]{1,0:T(8,128)(2,1)S(1)}, f32[1,512]{1,0:T(1,128)S(1)}, f32[1,512]{1,0:T(1,128)S(1)}, bf16[512...) custom-call(bf16[1024,512]{1,0:T(8,128)(2,1)S(1)} %bitcast.288, ...), custom_call_target="tpu_custom_call" | custom-call | flops 12884901888 | bytes 16777216 | tf_op jit(solution)/shard_map/pallas_call | solution.py:238
  85.0 5.2 %fusion.121 = (f32[512]{0:T(512)S(1)}, f32[512]{0:T(512)S(1)}, f32[512]{0:T(512)S(1)}, f32[512]{0:T(512)S(1)}, f32[512]{0:T(512)S(1)}, /*index=5*/f32[512]{0:T(5...) fusion(bf16[38,38,512]{2,1,0:T(8,128)(2,1)S(1)} %select_maximum, ...), kind=kLoop, calls=%fused_computation.220 | loop fusion | flops 28826624 | bytes 19959808 | tf_op jit(solution)/shard_map/reduce_sum | solution.py:123
  90.2 5.4 %fusion.103 = (f32[512]{0:T(512)S(1)}, f32[512]{0:T(512)S(1)}, f32[512]{0:T(512)S(1)}, f32[512]{0:T(512)S(1)}, f32[512]{0:T(512)S(1)}, /*index=5*/f32[512]{0:T(5...) fusion(bf16[38,38,512]{2,1,0:T(8,128)(2,1)S(1)} %select_maximum, ...), kind=kLoop, calls=%fused_computation.202 | loop fusion | flops 28826624 | bytes 19959808 | tf_op jit(solution)/shard_map/reduce_sum | solution.py:123
  96.0 4.1 %fusion.100 = (f32[512]{0:T(512)S(1)}, f32[512]{0:T(512)S(1)}, f32[512]{0:T(512)S(1)}, f32[512]{0:T(512)S(1)}, f32[512]{0:T(512)S(1)}, /*index=5*/f32[512]{0:T(5...) fusion(bf16[32,3,512]{2,1,0:T(4,128)(2,1)S(1)} %collective-perm, ...), kind=kLoop, calls=%fused_computation.199 | loop fusion | flops 28829696 | bytes 8609792 | tf_op jit(solution)/shard_map/reduce_sum | solution.py:123
  106.9 2.9 %collective-permute-start.12 = (bf16[32,3,512]{2,1,0:T(4,128)(2,1)S(1)}, bf16[32,3,512]{2,1,0:T(4,128)(2,1)S(1)}, u32[]{:S(2)}, u32[]{:S(2)}) collective-permute-start(bf16[32,3,512]{2,1,0:T(4,128)(2,1)S(1)} %get-tuple-element.96), channel_id=1, source_target_pairs={{0,1},{1,2},{2,3},{3,4},{4,5},{5,6},{6,7},{8,9},{9,10},{10,11},{11... | collective-permute-start | bytes 294920 | tf_op jit(solution)/shard_map/ppermute | solution.py:21
  111.2 2.7 %collective-permute-start.16 = (f32[58,512]{1,0:T(8,128)S(1)}, f32[58,512]{1,0:T(8,128)S(1)}, u32[]{:S(2)}, u32[]{:S(2)}) collective-permute-start(f32[58,512]{1,0:T(8,128)S(1)} %add.544), channel_id=1, source_target_pairs={{0,1},{1,0},{2,3},{3,2},{4,5},{5,4},{6,7},{7,6},{8,9},{9,8},{10,11... | collective-permute-start | bytes 356360 | tf_op jit(solution)/shard_map/ppermute | solution.py:45
  116.1 3.5 %collective-permute-done.16 = f32[58,512]{1,0:T(8,128)S(1)} collective-permute-done((f32[58,512]{1,0:T(8,128)S(1)}, f32[58,512]{1,0:T(8,128)S(1)}, u32[]{:S(2)}, u32[]{:S(2)}) %collective-permute-start.16) | collective-permute-done | bytes 118816 | tf_op jit(solution)/shard_map/ppermute | solution.py:45
  119.6 2.3 %collective-permute-start.17 = (f32[58,512]{1,0:T(8,128)S(1)}, f32[58,512]{1,0:T(8,128)S(1)}, u32[]{:S(2)}, u32[]{:S(2)}) collective-permute-start(f32[58,512]{1,0:T(8,128)S(1)} %add.545), channel_id=1, source_target_pairs={{0,2},{1,3},{2,0},{3,1},{4,6},{5,7},{6,4},{7,5},{8,10},{9,11},{10,... | collective-permute-start | bytes 356360 | tf_op jit(solution)/shard_map/ppermute | solution.py:45
  124.9 4.3 %collective-permute-start.18 = (f32[58,512]{1,0:T(8,128)S(1)}, f32[58,512]{1,0:T(8,128)S(1)}, u32[]{:S(2)}, u32[]{:S(2)}) collective-permute-start(f32[58,512]{1,0:T(8,128)S(1)} %add.546), channel_id=1, source_target_pairs={{0,4},{1,5},{2,6},{3,7},{4,0},{5,1},{6,2},{7,3},{8,12},{9,13},{10,... | collective-permute-start | bytes 356360 | tf_op jit(solution)/shard_map/ppermute | solution.py:45
  129.2 16.6 %fusion.132 = bf16[1,32,32,512]{3,2,1,0:T(8,128)(2,1)} fusion(bf16[38,38,512]{2,1,0:T(8,128)(2,1)S(1)} %select_maximum_fusion, f32[512]{0:T(512)S(1)} %bitcast.393, f32[512]{0:T(512)S(1)} %bitcast.395, f32[512]{0:T(512)S(1)} %bitcast.301, f32[512]{0:T(512)S(1)} %bitcast.303, f32[512]{0:T(512)S(1)} %bitcast.305, f32[512]{0:T(512)S(1)} %bitcast.307, ...), kind=kLoop, calls=%fused_computation.276 | loop fusion | flops 87556096 | bytes 47482880 | tf_op jit(solution)/shard_map/broadcast_in_dim | solution.py:339
  152.8 8.8 %collective-permute-done.25 = bf16[2,2,2,64,512]{4,3,1,2,0:T(8,128)(2,1)S(1)} collective-permute-done((bf16[2,2,2,64,512]{4,3,1,2,0:T(8,128)(2,1)S(1)}, bf16[2,2,2,64,512]{4,3,1,2,0:T(8,128)(2,1)S(1)}, u32[]{:S(2)}, u32[]{:S(2)}) %collective-permute-start.25) | collective-permute-done | bytes 524320 | tf_op jit(solution)/shard_map/ppermute | solution.py:45
  162.5 2.7 %collective-permute-done.20 = bf16[2,2,2,16,2048]{4,3,0,1,2:T(8,128)(2,1)S(1)} collective-permute-done((bf16[2,2,2,16,2048]{4,3,0,1,2:T(8,128)(2,1)S(1)}, bf16[2,2,2,16,2048]{4,3,0,1,2:T(8,128)(2,1)S(1)}, u32[]{:S(2)}, u32[]{:S(2)}) %collective-permute-start.20) | collective-permute-done | bytes 524320 | tf_op jit(solution)/shard_map/ppermute | solution.py:45
  167.1 2.4 %collective-permute-done.26 = bf16[2,2,64,512]{3,2,0,1:T(8,128)(2,1)S(1)} collective-permute-done((bf16[2,2,64,512]{3,2,0,1:T(8,128)(2,1)S(1)}, bf16[2,2,64,512]{3,2,0,1:T(8,128)(2,1)S(1)}, u32[]{:S(2)}, u32[]{:S(2)}) %collective-permute-start.26) | collective-permute-done | bytes 262176 | tf_op jit(solution)/shard_map/ppermute | solution.py:45
  172.7 2.3 %collective-permute-done.27 = bf16[2,64,512]{2,1,0:T(8,128)(2,1)S(1)} collective-permute-done((bf16[2,64,512]{2,1,0:T(8,128)(2,1)S(1)}, bf16[2,64,512]{2,1,0:T(8,128)(2,1)S(1)}, u32[]{:S(2)}, u32[]{:S(2)}) %collective-permute-start.27) | collective-permute-done | bytes 131104 | tf_op jit(solution)/shard_map/ppermute | solution.py:45
  175.5 2.5 %collective-permute-done.22 = bf16[2,16,2048]{2,1,0:T(8,128)(2,1)S(1)} collective-permute-done((bf16[2,16,2048]{2,1,0:T(8,128)(2,1)S(1)}, bf16[2,16,2048]{2,1,0:T(8,128)(2,1)S(1)}, u32[]{:S(2)}, u32[]{:S(2)}) %collective-permute-start.22) | collective-permute-done | bytes 131104 | tf_op jit(solution)/shard_map/ppermute | solution.py:45
  180.9 2.5 %collective-permute-done.23 = bf16[16,2048]{1,0:T(8,128)(2,1)S(1)} collective-permute-done((bf16[16,2048]{1,0:T(8,128)(2,1)S(1)}, bf16[16,2048]{1,0:T(8,128)(2,1)S(1)}, u32[]{:S(2)}, u32[]{:S(2)}) %collective-permute-start.23) | collective-permute-done | bytes 65568 | tf_op jit(solution)/shard_map/ppermute | solution.py:45
  (141 shorter events, 50.1 us)
Async XLA Ops:
  0.6 13.7 %collective-permute-start.7 = (bf16[64,512]{1,0:T(8,128)(2,1)}, bf16[64,512]{1,0:T(8,128)(2,1)S(1)}, u32[]{:S(2)}, u32[]{:S(2)}) collective-permute-start(bf16[64,512]{1,0:T(8,128)(2,1)} %param.19), channel_id=1, source_target_pairs={{0,4},{1,5},{2,6},{3,7},{4,0},{5,1},{6,2},{7,3},{8,12},{9,13},{10,... | collective-permute-start | bytes 196616 | tf_op jit(solution)/shard_map/ppermute | solution.py:45
  4.7 14.2 %collective-permute-start.2 = (bf16[16,2048]{1,0:T(8,128)(2,1)}, bf16[16,2048]{1,0:T(8,128)(2,1)S(1)}, u32[]{:S(2)}, u32[]{:S(2)}) collective-permute-start(bf16[16,2048]{1,0:T(8,128)(2,1)} %param.17), channel_id=1, source_target_pairs={{0,4},{1,5},{2,6},{3,7},{4,0},{5,1},{6,2},{7,3},{8,12},{9,13},{10,... | collective-permute-start | bytes 196616 | tf_op jit(solution)/shard_map/ppermute | solution.py:45
  6.0 29.9 %collective-permute-start = (bf16[32,3,512]{2,1,0:T(4,128)(2,1)S(1)}, bf16[32,3,512]{2,1,0:T(4,128)(2,1)S(1)}, u32[]{:S(2)}, u32[]{:S(2)}) collective-permute-start(bf16[32,3,512]{2,1,0:T(4,128)(2,1)S(1)} %get-tuple-element.102), channel_id=1, source_target_pairs={{0,1},{1,2},{2,3},{3,4},{4,5},{5,6},{6,7},{8,9},{9,10},{10,11},{11... | collective-permute-start | bytes 294920 | tf_op jit(solution)/shard_map/ppermute | solution.py:21
  9.7 26.2 %collective-permute-start.1 = (bf16[32,3,512]{2,1,0:T(4,128)(2,1)S(1)}, bf16[32,3,512]{2,1,0:T(4,128)(2,1)S(1)}, u32[]{:S(2)}, u32[]{:S(2)}) collective-permute-start(bf16[32,3,512]{2,1,0:T(4,128)(2,1)S(1)} %get-tuple-element.103), channel_id=1, source_target_pairs={{1,0},{2,1},{3,2},{4,3},{5,4},{6,5},{7,6},{9,8},{10,9},{11,10},{12... | collective-permute-start | bytes 294920 | tf_op jit(solution)/shard_map/ppermute | solution.py:22
  15.2 7.6 %collective-permute-start.8 = (bf16[2,64,512]{2,1,0:T(8,128)(2,1)S(1)}, bf16[2,64,512]{2,1,0:T(8,128)(2,1)S(1)}, u32[]{:S(2)}, u32[]{:S(2)}) collective-permute-start(bf16[2,64,512]{2,1,0:T(8,128)(2,1)S(1)} %pad_maximum_fusion.13), channel_id=1, source_target_pairs={{0,2},{1,3},{2,0},{3,1},{4,6},{5,7},{6,4},{7,5},{8,10},{9,11},{10,... | collective-permute-start | bytes 393224 | tf_op jit(solution)/shard_map/ppermute | solution.py:45
  22.9 6.4 %collective-permute-start.9 = (bf16[2,2,64,512]{3,2,0,1:T(8,128)(2,1)S(1)}, bf16[2,2,64,512]{3,2,0,1:T(8,128)(2,1)S(1)}, u32[]{:S(2)}, u32[]{:S(2)}) collective-permute-start(bf16[2,2,64,512]{3,2,0,1:T(8,128)(2,1)S(1)} %pad_maximum_fusion.11), channel_id=1, source_target_pairs={{0,16},{8,24},{16,0},{24,8},{1,17},{9,25},{17,1},{25,9},{2,18},{10... | collective-permute-start | bytes 786440 | tf_op jit(solution)/shard_map/ppermute | solution.py:45
  24.9 9.3 %collective-permute-start.4 = (bf16[2,2,16,2048]{3,2,0,1:T(8,128)(2,1)S(1)}, bf16[2,2,16,2048]{3,2,0,1:T(8,128)(2,1)S(1)}, u32[]{:S(2)}, u32[]{:S(2)}) collective-permute-start(bf16[2,2,16,2048]{3,2,0,1:T(8,128)(2,1)S(1)} %pad_maximum_fusion.10), channel_id=1, source_target_pairs={{0,1},{1,0},{2,3},{3,2},{4,5},{5,4},{6,7},{7,6},{8,9},{9,8},{10,11... | collective-permute-start | bytes 786440 | tf_op jit(solution)/shard_map/ppermute | solution.py:45
  29.5 13.2 %collective-permute-start.10 = (bf16[2,2,2,64,512]{4,3,1,2,0:T(8,128)(2,1)S(1)}, bf16[2,2,2,64,512]{4,3,1,2,0:T(8,128)(2,1)S(1)}, u32[]{:S(2)}, u32[]{:S(2)}) collective-permute-start(bf16[2,2,2,64,512]{4,3,1,2,0:T(8,128)(2,1)S(1)} %pad_maximum_fusion.9), channel_id=1, source_target_pairs={{0,1},{1,0},{2,3},{3,2},{4,5},{5,4},{6,7},{7,6},{8,9},{9,8},{10,11... | collective-permute-start | bytes 1572872 | tf_op jit(solution)/shard_map/ppermute | solution.py:45
  34.3 9.2 %collective-permute-start.5 = (bf16[2,2,2,16,2048]{4,3,0,1,2:T(8,128)(2,1)S(1)}, bf16[2,2,2,16,2048]{4,3,0,1,2:T(8,128)(2,1)S(1)}, u32[]{:S(2)}, u32[]{:S(2)}) collective-permute-start(bf16[2,2,2,16,2048]{4,3,0,1,2:T(8,128)(2,1)S(1)} %pad_maximum_fusion.8), channel_id=1, source_target_pairs={{0,16},{8,24},{16,0},{24,8},{1,17},{9,25},{17,1},{25,9},{2,18},{10... | collective-permute-start | bytes 1572872 | tf_op jit(solution)/shard_map/ppermute | solution.py:45
  42.9 17.1 %collective-permute-start.11 = (bf16[2,2,2,2,64,512]{5,4,1,2,0,3:T(8,128)(2,1)S(1)}, bf16[2,2,2,2,64,512]{5,4,1,2,0,3:T(8,128)(2,1)S(1)}, u32[]{:S(2)}, u32[]{:S(2)}) collective-permute-start(bf16[2,2,2,2,64,512]{5,4,1,2,0,3:T(8,128)(2,1)S(1)} %pad_maximum_fusion.7), channel_id=1, source_target_pairs={{0,8},{8,0},{16,24},{24,16},{1,9},{9,1},{17,25},{25,17},{2,10},{10... | collective-permute-start | bytes 3145736 | tf_op jit(solution)/shard_map/ppermute | solution.py:45
  43.7 18.0 %collective-permute-start.6 = (bf16[2,2,2,2,16,2048]{5,4,1,2,3,0:T(8,128)(2,1)S(1)}, bf16[2,2,2,2,16,2048]{5,4,1,2,3,0:T(8,128)(2,1)S(1)}, u32[]{:S(2)}, u32[]{:S(2)}) collective-permute-start(bf16[2,2,2,2,16,2048]{5,4,1,2,3,0:T(8,128)(2,1)S(1)} %pad_maximum_fusion.6), channel_id=1, source_target_pairs={{0,8},{8,0},{16,24},{24,16},{1,9},{9,1},{17,25},{25,17},{2,10},{10... | collective-permute-start | bytes 3145736 | tf_op jit(solution)/shard_map/ppermute | solution.py:45
  104.9 42.2 %collective-permute-start.24 = (bf16[2,2,2,2,64,512]{5,4,1,2,0,3:T(8,128)(2,1)}, bf16[2,2,2,2,64,512]{5,4,1,2,0,3:T(8,128)(2,1)}, u32[]{:S(2)}, u32[]{:S(2)}) collective-permute-start(bf16[2,2,2,2,64,512]{5,4,1,2,0,3:T(8,128)(2,1)} %bitcast.277), channel_id=1, source_target_pairs={{0,8},{8,0},{16,24},{24,16},{1,9},{9,1},{17,25},{25,17},{2,10},{10... | collective-permute-start | bytes 3145736 | tf_op jit(solution)/shard_map/ppermute | solution.py:45
  105.2 5.9 %collective-permute-start.15 = (f32[58,512]{1,0:T(8,128)S(1)}, f32[58,512]{1,0:T(8,128)S(1)}, u32[]{:S(2)}, u32[]{:S(2)}) collective-permute-start(f32[58,512]{1,0:T(8,128)S(1)} %add.543), channel_id=1, source_target_pairs={{0,16},{8,24},{16,0},{24,8},{1,17},{9,25},{17,1},{25,9},{2,18},{10... | collective-permute-start | bytes 356360 | tf_op jit(solution)/shard_map/ppermute | solution.py:45
  106.9 15.0 %collective-permute-start.12 = (bf16[32,3,512]{2,1,0:T(4,128)(2,1)S(1)}, bf16[32,3,512]{2,1,0:T(4,128)(2,1)S(1)}, u32[]{:S(2)}, u32[]{:S(2)}) collective-permute-start(bf16[32,3,512]{2,1,0:T(4,128)(2,1)S(1)} %get-tuple-element.96), channel_id=1, source_target_pairs={{0,1},{1,2},{2,3},{3,4},{4,5},{5,6},{6,7},{8,9},{9,10},{10,11},{11... | collective-permute-start | bytes 294920 | tf_op jit(solution)/shard_map/ppermute | solution.py:21
  109.8 12.1 %collective-permute-start.13 = (bf16[32,3,512]{2,1,0:T(4,128)(2,1)S(1)}, bf16[32,3,512]{2,1,0:T(4,128)(2,1)S(1)}, u32[]{:S(2)}, u32[]{:S(2)}) collective-permute-start(bf16[32,3,512]{2,1,0:T(4,128)(2,1)S(1)} %get-tuple-element.97), channel_id=1, source_target_pairs={{1,0},{2,1},{3,2},{4,3},{5,4},{6,5},{7,6},{9,8},{10,9},{11,10},{12... | collective-permute-start | bytes 294920 | tf_op jit(solution)/shard_map/ppermute | solution.py:22
  111.2 8.4 %collective-permute-start.16 = (f32[58,512]{1,0:T(8,128)S(1)}, f32[58,512]{1,0:T(8,128)S(1)}, u32[]{:S(2)}, u32[]{:S(2)}) collective-permute-start(f32[58,512]{1,0:T(8,128)S(1)} %add.544), channel_id=1, source_target_pairs={{0,1},{1,0},{2,3},{3,2},{4,5},{5,4},{6,7},{7,6},{8,9},{9,8},{10,11... | collective-permute-start | bytes 356360 | tf_op jit(solution)/shard_map/ppermute | solution.py:45
  116.1 33.6 %collective-permute-start.19 = (bf16[2,2,2,2,16,2048]{5,4,1,2,3,0:T(8,128)(2,1)}, bf16[2,2,2,2,16,2048]{5,4,1,2,3,0:T(8,128)(2,1)}, u32[]{:S(2)}, u32[]{:S(2)}) collective-permute-start(bf16[2,2,2,2,16,2048]{5,4,1,2,3,0:T(8,128)(2,1)} %bitcast.278), channel_id=1, source_target_pairs={{0,8},{8,0},{16,24},{24,16},{1,9},{9,1},{17,25},{25,17},{2,10},{10... | collective-permute-start | bytes 3145736 | tf_op jit(solution)/shard_map/ppermute | solution.py:45
  124.9 20.9 %collective-permute-start.18 = (f32[58,512]{1,0:T(8,128)S(1)}, f32[58,512]{1,0:T(8,128)S(1)}, u32[]{:S(2)}, u32[]{:S(2)}) collective-permute-start(f32[58,512]{1,0:T(8,128)S(1)} %add.546), channel_id=1, source_target_pairs={{0,4},{1,5},{2,6},{3,7},{4,0},{5,1},{6,2},{7,3},{8,12},{9,13},{10,... | collective-permute-start | bytes 356360 | tf_op jit(solution)/shard_map/ppermute | solution.py:45
  148.8 12.8 %collective-permute-start.25 = (bf16[2,2,2,64,512]{4,3,1,2,0:T(8,128)(2,1)S(1)}, bf16[2,2,2,64,512]{4,3,1,2,0:T(8,128)(2,1)S(1)}, u32[]{:S(2)}, u32[]{:S(2)}) collective-permute-start(bf16[2,2,2,64,512]{4,3,1,2,0:T(8,128)(2,1)S(1)} %fusion.134), channel_id=1, source_target_pairs={{0,1},{1,0},{2,3},{3,2},{4,5},{5,4},{6,7},{7,6},{8,9},{9,8},{10,11... | collective-permute-start | bytes 1572872 | tf_op jit(solution)/shard_map/ppermute | solution.py:45
  151.4 13.8 %collective-permute-start.20 = (bf16[2,2,2,16,2048]{4,3,0,1,2:T(8,128)(2,1)S(1)}, bf16[2,2,2,16,2048]{4,3,0,1,2:T(8,128)(2,1)S(1)}, u32[]{:S(2)}, u32[]{:S(2)}) collective-permute-start(bf16[2,2,2,16,2048]{4,3,0,1,2:T(8,128)(2,1)S(1)} %fusion.133), channel_id=1, source_target_pairs={{0,16},{8,24},{16,0},{24,8},{1,17},{9,25},{17,1},{25,9},{2,18},{10... | collective-permute-start | bytes 1572872 | tf_op jit(solution)/shard_map/ppermute | solution.py:45
  161.8 7.6 %collective-permute-start.26 = (bf16[2,2,64,512]{3,2,0,1:T(8,128)(2,1)S(1)}, bf16[2,2,64,512]{3,2,0,1:T(8,128)(2,1)S(1)}, u32[]{:S(2)}, u32[]{:S(2)}) collective-permute-start(bf16[2,2,64,512]{3,2,0,1:T(8,128)(2,1)S(1)} %fusion.136), channel_id=1, source_target_pairs={{0,16},{8,24},{16,0},{24,8},{1,17},{9,25},{17,1},{25,9},{2,18},{10... | collective-permute-start | bytes 786440 | tf_op jit(solution)/shard_map/ppermute | solution.py:45
  165.4 6.4 %collective-permute-start.21 = (bf16[2,2,16,2048]{3,2,0,1:T(8,128)(2,1)S(1)}, bf16[2,2,16,2048]{3,2,0,1:T(8,128)(2,1)S(1)}, u32[]{:S(2)}, u32[]{:S(2)}) collective-permute-start(bf16[2,2,16,2048]{3,2,0,1:T(8,128)(2,1)S(1)} %fusion.135), channel_id=1, source_target_pairs={{0,1},{1,0},{2,3},{3,2},{4,5},{5,4},{6,7},{7,6},{8,9},{9,8},{10,11... | collective-permute-start | bytes 786440 | tf_op jit(solution)/shard_map/ppermute | solution.py:45
  171.9 6.0 %collective-permute-start.22 = (bf16[2,16,2048]{2,1,0:T(8,128)(2,1)S(1)}, bf16[2,16,2048]{2,1,0:T(8,128)(2,1)S(1)}, u32[]{:S(2)}, u32[]{:S(2)}) collective-permute-start(bf16[2,16,2048]{2,1,0:T(8,128)(2,1)S(1)} %fusion.137), channel_id=1, source_target_pairs={{0,2},{1,3},{2,0},{3,1},{4,6},{5,7},{6,4},{7,5},{8,10},{9,11},{10,... | collective-permute-start | bytes 393224 | tf_op jit(solution)/shard_map/ppermute | solution.py:45
  178.0 5.4 %collective-permute-start.23 = (bf16[16,2048]{1,0:T(8,128)(2,1)S(1)}, bf16[16,2048]{1,0:T(8,128)(2,1)S(1)}, u32[]{:S(2)}, u32[]{:S(2)}) collective-permute-start(bf16[16,2048]{1,0:T(8,128)(2,1)S(1)} %fusion.139), channel_id=1, source_target_pairs={{0,4},{1,5},{2,6},{3,7},{4,0},{5,1},{6,2},{7,3},{8,12},{9,13},{10,... | collective-permute-start | bytes 196616 | tf_op jit(solution)/shard_map/ppermute | solution.py:45
  (15 other events, 58.5 us)

commit v3 on v2

--- a/solution.py
+++ b/solution.py
@@ -49,42 +49,44 @@
     return (lax.axis_index(key[0]) // key[1]) % 2
 
 
-def gather_rows(x, other_order=False):
-    tail = x.shape[1]
-    present = []
-    for key in index_bits(other_order)[::-1]:
-        other = swapped(x, key)
-        present = sorted(present + [key], key=row_order)
-        at = present.index(key)
-        high = own_bit(key) == 1
-        x = jnp.stack([jnp.where(high, other, x), jnp.where(high, x, other)], axis=at)
-    return x.reshape(-1, tail)
-
-
-def scatter_sum_rows(x, other_order=False):
-    keys = index_bits(other_order)
-    present = sorted(keys, key=row_order)
-    x = x.reshape((2,) * len(keys) + (-1, x.shape[1]))
-    for key in keys:
-        at = present.index(key)
-        bit = own_bit(key)
-        kept = lax.dynamic_index_in_dim(x, bit, at, keepdims=False)
-        sent = lax.dynamic_index_in_dim(x, 1 - bit, at, keepdims=False).astype(jnp.bfloat16)
-        x = kept.astype(jnp.float32) + swapped(sent, key).astype(jnp.float32)
-        present.remove(key)
-    return x
-
-
-def sum_everywhere(parts):
-    flat = jnp.concatenate([part.reshape(-1, parts[0].shape[-1]) for part in parts])
-    for key in index_bits():
-        flat = flat + swapped(flat, key)
-    outs, at = [], 0
-    for part in parts:
-        rows = part.size // flat.shape[1]
-        outs.append(flat[at : at + rows].reshape(part.shape))
-        at += rows
-    return outs
+def gather_step(x, other, present, key):
+    present.append(key)
+    present.sort(key=row_order)
+    high = own_bit(key) == 1
+    return jnp.stack(
+        [jnp.where(high, other, x), jnp.where(high, x, other)], axis=present.index(key)
+    )
+
+
+def halves(x, present, key):
+    at = present.index(key)
+    bit = own_bit(key)
+    present.remove(key)
+    kept = lax.dynamic_index_in_dim(x, bit, at, keepdims=False).astype(jnp.float32)
+    sent = lax.dynamic_index_in_dim(x, 1 - bit, at, keepdims=False).astype(jnp.bfloat16)
+    return kept, sent
+
+
+def tied(*values):
+    return lax.optimization_barrier(values)
+
+
+def gather_beside(weight_in, weight_out, source, works):
+    in_keys, out_keys = index_bits()[::-1], index_bits(True)[::-1]
+    in_present, out_present, done = [], [], []
+    first, second = weight_in, weight_out
+    for k, (in_key, out_key) in enumerate(zip(in_keys, out_keys)):
+        place = k - (len(in_keys) - len(works))
+        if place >= 0:
+            first, second, source = tied(first, second, source)
+        first_other, second_other = swapped(first, in_key), swapped(second, out_key)
+        if place >= 0:
+            result = works[place](source)
+            first_other, second_other, result = tied(first_other, second_other, result)
+            done.append(result)
+        first = gather_step(first, first_other, in_present, in_key)
+        second = gather_step(second, second_other, out_present, out_key)
+    return first.reshape(-1, weight_in.shape[1]), second.reshape(-1, weight_out.shape[1]), done
 
 
 def conv_forward(padded, kernel, offset, row_count, col_count):
@@ -111,18 +113,16 @@
     return summed
 
 
-def kernel_gradient(grad_conv, padded, row_count, col_count):
+def kernel_gradient(grad_conv, padded, row_count, col_count, tap_rows):
     grad_wide = grad_conv.astype(jnp.float32)
     taps = []
-    for tap_row in range(KS):
-        tap_line = []
+    for tap_row in tap_rows:
         for tap_col in range(KS):
             window = padded[tap_row : tap_row + row_count, tap_col : tap_col + col_count].astype(
                 jnp.float32
             )
-            tap_line.append(jnp.sum(grad_wide * window, axis=(0, 1)))
-        taps.append(jnp.stack(tap_line))
-    return jnp.stack(taps)
+            taps.append(jnp.sum(grad_wide * window, axis=(0, 1)))
+    return taps
 
 
 def dot(a, b, over_a, over_b):
@@ -295,13 +295,19 @@
     source = features[0]
     upstream = cotangent[0]
     row_count, col_count, channels = source.shape
-    full_in, full_out = (
-        gather_rows(weight_in),
-        gather_rows(weight_out, True),
-    )
     rimmed = padded_2(source, (("space", 1),), reach)
     padded = jnp.pad(rimmed, ((reach, reach), (0, 0), (0, 0)))
-    conv_out = conv_forward(padded, conv_kernel, conv_bias, row_count, col_count)
+    half = row_count // 2
+
+    def conv_rows(start):
+        return lambda x: conv_forward(
+            x[start : start + half + KS - 1], conv_kernel, conv_bias, half, col_count
+        )
+
+    full_in, full_out, conv_halves = gather_beside(
+        weight_in, weight_out, padded, (conv_rows(0), conv_rows(half))
+    )
+    conv_out = jnp.concatenate(conv_halves)
     block_out, grad_conv, *partials = norm_mlp(
         conv_out.reshape(-1, channels),
         source.reshape(-1, channels),
@@ -317,9 +323,6 @@
     grad_conv = grad_conv.reshape(row_count, col_count, channels)
     grad_rimmed = padded_2(grad_conv, (("space", 1),), reach)
     grad_padded = jnp.pad(grad_rimmed, ((reach, reach), (0, 0), (0, 0)))
-    conv_back = conv_backward(grad_padded, conv_kernel, row_count, col_count)
-    grad_kern = kernel_gradient(grad_conv, padded, row_count, col_count)
-    grad_feat = (upstream.astype(jnp.float32) + conv_back).astype(jnp.bfloat16)
     (
         grad_gain,
         grad_normbias,
@@ -330,10 +333,63 @@
         grad_scale,
         grad_cbias,
     ) = partials
-    reduced = sum_everywhere(
-        (grad_kern, grad_cbias, grad_gain, grad_normbias, grad_inbias, grad_outbias, grad_scale)
-    )
-    owned_in, owned_out = (scatter_sum_rows(grad_inproj), scatter_sum_rows(grad_outproj, True))
+    in_keys, out_keys = index_bits(), index_bits(True)
+    in_present, out_present = sorted(in_keys, key=row_order), sorted(out_keys, key=row_order)
+    first = grad_inproj.reshape((2,) * len(in_keys) + (-1, grad_inproj.shape[1]))
+    second = grad_outproj.reshape((2,) * len(out_keys) + (-1, channels))
+    small_keys = list(in_keys)
+    small = None
+    taps, back = [], []
+    for k, (in_key, out_key) in enumerate(zip(in_keys, out_keys)):
+        first_kept, first_sent = halves(first, in_present, in_key)
+        second_kept, second_sent = halves(second, out_present, out_key)
+        if k < 2:
+            first_sent, second_sent, g, p = tied(first_sent, second_sent, grad_conv, padded)
+            first_got, second_got = swapped(first_sent, in_key), swapped(second_sent, out_key)
+            rows = range(2) if k == 0 else range(2, KS)
+            result = kernel_gradient(g, p, row_count, col_count, rows)
+            first_got, second_got, result = tied(first_got, second_got, result)
+            taps += result
+            if k == 1:
+                parts = (
+                    grad_cbias,
+                    grad_gain,
+                    grad_normbias,
+                    grad_inbias,
+                    grad_outbias,
+                    grad_scale,
+                )
+                small = jnp.concatenate(
+                    [jnp.stack(taps)] + [part.reshape(-1, channels) for part in parts]
+                )
+        else:
+            first_sent, second_sent, small, p = tied(first_sent, second_sent, small, grad_padded)
+            first_got, second_got = swapped(first_sent, in_key), swapped(second_sent, out_key)
+            small_got = swapped(small, small_keys.pop(0))
+            result = ()
+            if k < 4:
+                start = (k - 2) * half
+                window = p[start : start + half + KS - 1]
+                wide = conv_backward(window, conv_kernel, half, col_count)
+                wide = wide + upstream[start : start + half].astype(jnp.float32)
+                result = wide.astype(jnp.bfloat16)
+            first_got, second_got, small_got, result = tied(
+                first_got, second_got, small_got, result
+            )
+            small = small + small_got
+            if k < 4:
+                back.append(result)
+        first = first_kept + first_got.astype(jnp.float32)
+        second = second_kept + second_got.astype(jnp.float32)
+    for key in small_keys:
+        small = small + swapped(small, key)
+    owned_in, owned_out = first, second
+    grad_feat = jnp.concatenate(back)
+    reduced, at = [small[: KS * KS].reshape(KS, KS, channels)], KS * KS
+    for part in parts:
+        rows = part.size // channels
+        reduced.append(small[at : at + rows])
+        at += rows
     return (
         block_out.reshape(1, row_count, col_count, channels),
         grad_feat[None],

time: 185 us -> 176 us (0.951)
  waiting for transfers between devices: 47 us -> 24.6 us
  local copies, waits for them, and re-layouts: 15.6 us -> 26.6 us
  other arithmetic: 58.2 us -> 60.3 us
    ppermute x25, waiting for transfers between devices: 46.9 us -> 24.6 us  [swapped(): lax.ppermute(x, axis, [(i, i ^ stride) for i in range(lax.axis_size(axis))])]
    convert_element_type x0 -> x2, other arithmetic: none -> 15.6 us  [local(): result = wide.astype(jnp.bfloat16)]
    broadcast_in_dim x1, other arithmetic: 16.6 us -> 1.06 us  [local(): grad_feat[None]]
    concatenate x1, local copies, waits for them, and re-layouts: 0.06 us -> 4.45 us  [local(): jnp.concatenate([jnp.stack(taps)] + [part.reshape(-1, channels) for part...]
    unnamed x28 -> x156, local copies, waits for them, and re-layouts: 0.69 us -> 3.15 us
    reduce_sum x4 -> x3, other arithmetic: 15.2 us -> 16.1 us  [kernel_gradient(): taps.append(jnp.sum(grad_wide * window, axis=(0, 1)))]
    convert_element_type x1 -> x2, other arithmetic: 16.1 us -> 15.3 us  [conv_forward(): return (summed + offset).astype(jnp.bfloat16)]
  transfers between devices with their start and end apart: 29 -> 29, of which waited for: 16 -> 11; matrix products, arithmetic and copies ran while one was open for 30% -> 38% of each run, Pallas kernels for 0% -> 0%
where the time goes in v3:
time: 176 us; the launch traced here: 175 us
  other arithmetic  60.3 us (34%)
  starting transfers between devices  40 us (23%)
  local copies, waits for them, and re-layouts  26.6 us (15%)
  waiting for transfers between devices  24.6 us (14%)
  Pallas kernels  21.2 us (12%)
  between operations  2.3 us (1%)
    ppermute x25, starting transfers between devices, swapped(): lax.ppermute(x, axis, [(i, i ^ stride) for i in range(lax.axis_size(axis))])  29.9 us
    ppermute x25, waiting for transfers between devices, swapped(): lax.ppermute(x, axis, [(i, i ^ stride) for i in range(lax.axis_size(axis))])  24.6 us
    pallas_call x1, Pallas kernels, norm_mlp(): pl.pallas_call(norm_mlp_kernel, grid=(units // tile,), in_specs=[whole, w...  21.2 us
    reduce_sum x3, other arithmetic, kernel_gradient(): taps.append(jnp.sum(grad_wide * window, axis=(0, 1)))  16.1 us
    convert_element_type x2, other arithmetic, local(): result = wide.astype(jnp.bfloat16)  15.6 us
    convert_element_type x2, other arithmetic, conv_forward(): return (summed + offset).astype(jnp.bfloat16)  15.3 us
    ppermute x2, starting transfers between devices, padded_2(): before = lax.ppermute(last, axis, up)  7.32 us
    concatenate x1, local copies, waits for them, and re-layouts, local(): jnp.concatenate([jnp.stack(taps)] + [part.reshape(-1, channels) for part...  4.45 us
  transfers between devices with their start and end apart: 29, of which 11 were waited for; matrix products, arithmetic and copies ran while one was open for 38% of the time, Pallas kernels for 0%

profile of v3, /device:TPU:0, one launch (start us, length us, event | category | flops | bytes accessed | tf_op | source)
XLA Modules:
  0.0 175.1 jit_solution(171845524788266955)
XLA Ops:
  0.7 4.1 %collective-permute-start.3 = (bf16[64,512]{1,0:T(8,128)(2,1)}, bf16[64,512]{1,0:T(8,128)(2,1)S(1)}, u32[]{:S(2)}, u32[]{:S(2)}) collective-permute-start(bf16[64,512]{1,0:T(8,128)(2,1)} %param.19), channel_id=1, source_target_pairs={{0,4},{1,5},{2,6},{3,7},{4,0},{5,1},{6,2},{7,3},{8,12},{9,13},{10,... | collective-permute-start | bytes 196616 | tf_op jit(solution)/shard_map/ppermute | solution.py:45
  6.0 3.7 %collective-permute-start.6 = (bf16[32,3,512]{2,1,0:T(4,128)(2,1)S(1)}, bf16[32,3,512]{2,1,0:T(4,128)(2,1)S(1)}, u32[]{:S(2)}, u32[]{:S(2)}) collective-permute-start(bf16[32,3,512]{2,1,0:T(4,128)(2,1)S(1)} %get-tuple-element.284), channel_id=1, source_target_pairs={{0,1},{1,2},{2,3},{3,4},{4,5},{5,6},{6,7},{8,9},{9,10},{10,11},{11... | collective-permute-start | bytes 294920 | tf_op jit(solution)/shard_map/ppermute | solution.py:21
  15.3 3.7 %collective-permute-start.4 = (bf16[2,64,512]{2,1,0:T(8,128)(2,1)S(1)}, bf16[2,64,512]{2,1,0:T(8,128)(2,1)S(1)}, u32[]{:S(2)}, u32[]{:S(2)}) collective-permute-start(bf16[2,64,512]{2,1,0:T(8,128)(2,1)S(1)} %pad_maximum_fusion.10), channel_id=1, source_target_pairs={{0,2},{1,3},{2,0},{3,1},{4,6},{5,7},{6,4},{7,5},{8,10},{9,11},{10,... | collective-permute-start | bytes 393224 | tf_op jit(solution)/shard_map/ppermute | solution.py:45
  20.8 2.2 %collective-permute-done.4 = bf16[2,64,512]{2,1,0:T(8,128)(2,1)S(1)} collective-permute-done((bf16[2,64,512]{2,1,0:T(8,128)(2,1)S(1)}, bf16[2,64,512]{2,1,0:T(8,128)(2,1)S(1)}, u32[]{:S(2)}, u32[]{:S(2)}) %collective-permute-start.4) | collective-permute-done | bytes 131104 | tf_op jit(solution)/shard_map/ppermute | solution.py:45
  26.2 3.3 %collective-permute-done.5 = bf16[2,2,64,512]{3,2,0,1:T(8,128)(2,1)S(1)} collective-permute-done((bf16[2,2,64,512]{3,2,0,1:T(8,128)(2,1)S(1)}, bf16[2,2,64,512]{3,2,0,1:T(8,128)(2,1)S(1)}, u32[]{:S(2)}, u32[]{:S(2)}) %collective-permute-start.5) | collective-permute-done | bytes 262176 | tf_op jit(solution)/shard_map/ppermute | solution.py:45
  29.6 2.0 %collective-permute-done.2 = bf16[2,2,16,2048]{3,2,0,1:T(8,128)(2,1)S(1)} collective-permute-done((bf16[2,2,16,2048]{3,2,0,1:T(8,128)(2,1)S(1)}, bf16[2,2,16,2048]{3,2,0,1:T(8,128)(2,1)S(1)}, u32[]{:S(2)}, u32[]{:S(2)}) %collective-permute-start.2) | collective-permute-done | bytes 262176 | tf_op jit(solution)/shard_map/ppermute | solution.py:45
  34.5 7.6 %add_convert_fusion.1 = bf16[16,32,512]{2,1,0:T(8,128)(2,1)S(1)} fusion(f32[512]{0:T(512)S(1)} %copy-done.58, bf16[38,38,512]{2,1,0:T(8,128)(2,1)S(1)} %select_maximum_fusion.2, f32[512]{0:T(512)S(1)} %bitcast.424, f32[512]{0:T(512)S(1)} %bitcast.428, f32[512]{0:T(512)S(1)} %bitcast.240, f32[512]{0:T(512)S(1)} %bitcast.244, f32[512]{0:T(512)S(1)} %bitcast.248, ...), kind=kLoop, calls=%fused_computation.131 | loop fusion | flops 38797312 | bytes 26316800 | tf_op jit(solution)/shard_map/convert_element_type | solution.py:100
  45.3 7.7 %add_convert_fusion = bf16[16,32,512]{2,1,0:T(8,128)(2,1)S(1)} fusion(bf16[38,38,512]{2,1,0:T(8,128)(2,1)S(1)} %select_maximum_fusion.2, f32[512]{0:T(512)S(1)} %copy-done.58, f32[512]{0:T(512)S(1)} %bitcast.425, f32[512]{0:T(512)S(1)} %bitcast.429, f32[512]{0:T(512)S(1)} %bitcast.241, f32[512]{0:T(512)S(1)} %bitcast.245, f32[512]{0:T(512)S(1)} %bitcast.249, ...), kind=kLoop, calls=%fused_computation.130 | loop fusion | flops 38797312 | bytes 26316800 | tf_op jit(solution)/shard_map/convert_element_type | solution.py:100
  58.0 21.2 %shard_map.194 = (bf16[1024,512]{1,0:T(8,128)(2,1)}, bf16[1024,512]{1,0:T(8,128)(2,1)S(1)}, f32[1,512]{1,0:T(1,128)S(1)}, f32[1,512]{1,0:T(1,128)S(1)}, bf16[512...) custom-call(bf16[1024,512]{1,0:T(8,128)(2,1)S(1)} %bitcast.226, ...), custom_call_target="tpu_custom_call" | custom-call | flops 12884901888 | bytes 16777216 | tf_op jit(solution)/shard_map/pallas_call | solution.py:238
  80.0 3.6 %collective-permute-start.16 = (bf16[32,3,512]{2,1,0:T(4,128)(2,1)}, bf16[32,3,512]{2,1,0:T(4,128)(2,1)S(1)}, u32[]{:S(2)}, u32[]{:S(2)}) collective-permute-start(bf16[32,3,512]{2,1,0:T(4,128)(2,1)} %get-tuple-element.278), channel_id=1, source_target_pairs={{0,1},{1,2},{2,3},{3,4},{4,5},{5,6},{6,7},{8,9},{9,10},{10,11},{11... | collective-permute-start | bytes 294920 | tf_op jit(solution)/shard_map/ppermute | solution.py:21
  85.2 2.7 %constant_dynamic-slice_fusion = (bf16[2,1,2,2,2,64,512]{6,5,4,3,2,1,0:T(8,128)(2,1)}, bf16[2,1,2,2,2,64,512]{6,5,4,3,2,1,0:T(8,128)(2,1)S(1)}) fusion(bf16[2,2,2,2,2,64,512]{6,5,4,3,2,1,0:T(8,128)(2,1)} %bitcast.233, s32[]{:T(128)S(6)} %select_n.288, s32[]{:T(128)S(6)} %select_n.289), kind=kLoop, calls=%fused_computation.175 | loop fusion | bytes 4194312 | tf_op jit(solution)/shard_map/jit(dynamic_index_in_dim)/dynamic_slice | solution.py:65
  92.6 4.6 %fusion.14 = (f32[512]{0:T(512)}, f32[512]{0:T(512)}, f32[512]{0:T(512)}, f32[512]{0:T(512)}, f32[512]{0:T(512)}, /*index=5*/f32[512]{0:T(512)}, f32[512]{0:T(51...) fusion(bf16[32,32,512]{2,1,0:T(8,128)(2,1)S(1)} %bitcast.218, ...), kind=kLoop, calls=%fused_computation.65 | loop fusion | flops 22537216 | bytes 15757312 | tf_op jit(solution)/shard_map/reduce_sum | solution.py:124
  100.3 1.9 %select_maximum_fusion = bf16[38,38,512]{2,1,0:T(8,128)(2,1)} fusion(bf16[32,3,512]{2,1,0:T(4,128)(2,1)S(1)} %collective-permute-done.17, bf16[32,32,512]{2,1,0:T(8,128)(2,1)S(1)} %bitcast.219, bf16[32,3,512]{2,1,0:T(4,128)(2,1)S(1)} %collective-permute-done.16), kind=kLoop, calls=%fused_computation.105 | loop fusion | flops 8871936 | bytes 2723840 | tf_op jit(solution)/shard_map/concatenate | solution.py:23
  106.2 2.6 %collective-permute-start.15 = (bf16[2,2,2,64,512]{4,3,1,2,0:T(8,128)(2,1)S(1)}, bf16[2,2,2,64,512]{4,3,1,2,0:T(8,128)(2,1)S(1)}, u32[]{:S(2)}, u32[]{:S(2)}) collective-permute-start(bf16[2,2,2,64,512]{4,3,1,2,0:T(8,128)(2,1)S(1)} %fusion.54), channel_id=1, source_target_pairs={{0,1},{1,0},{2,3},{3,2},{4,5},{5,4},{6,7},{7,6},{8,9},{9,8},{10,11... | collective-permute-start | bytes 1572872 | tf_op jit(solution)/shard_map/ppermute | solution.py:45
  108.8 6.0 %fusion.49 = (f32[512]{0:T(512)}, f32[512]{0:T(512)}, f32[512]{0:T(512)}, f32[512]{0:T(512)}, f32[512]{0:T(512)}, /*index=5*/f32[512]{0:T(512)}, f32[512]{0:T(51...) fusion(bf16[32,32,512]{2,1,0:T(8,128)(2,1)S(1)} %bitcast.220, ...), kind=kLoop, calls=%fused_computation.100 | loop fusion | flops 28826624 | bytes 19959808 | tf_op jit(solution)/shard_map/reduce_sum | solution.py:124
  114.8 5.5 %fusion.48 = (f32[512]{0:T(512)S(1)}, f32[512]{0:T(512)S(1)}, f32[512]{0:T(512)}, f32[512]{0:T(512)}, f32[512]{0:T(512)}, /*index=5*/f32[512]{0:T(512)}, f32[512...) fusion(bf16[32,32,512]{2,1,0:T(8,128)(2,1)S(1)} %bitcast.221, ...), kind=kLoop, calls=%fused_computation.99 | loop fusion | flops 27254272 | bytes 18909184 | tf_op jit(solution)/shard_map/reduce_sum | solution.py:124
  123.3 4.5 %concatenate.17 = f32[58,512]{1,0:T(8,128)S(1)} concatenate(f32[1,512]{1,0:T(1,128)S(1)} %bitcast.445, f32[1,512]{1,0:T(1,128)S(1)} %bitcast.433, f32[1,512]{1,0:T(1,128)S(1)} %bitcast.434, f32[1,512]{1,0:T(1,128)S(1)} %bitcast.435, f32[1,512]{1,0:T(1,128)S(1)} %bitcast.436, f32[1,512]{1,0:T(1,128)S(1)} %bitcast.437, f32[1,512]{1,0:T(1,128)S(1)} %bitcast.438, ...), dimensions={0} | concatenate | bytes 237568 | tf_op jit(solution)/shard_map/concatenate | solution.py:362
  131.5 7.9 %fusion.52 = bf16[16,32,512]{2,1,0:T(8,128)(2,1)S(1)} fusion(bf16[1,32,32,512]{3,2,1,0:T(8,128)(2,1)S(1)} %copy-done.1, bf16[38,38,512]{2,1,0:T(8,128)(2,1)S(1)} %copy-done.9, f32[512]{0:T(512)S(1)} %bitcast.426, f32[512]{0:T(512)S(1)} %bitcast.430, f32[512]{0:T(512)S(1)} %bitcast.242, f32[512]{0:T(512)S(1)} %bitcast.246, f32[512]{0:T(512)S(1)} %bitcast.250, ...), kind=kLoop, calls=%fused_computation.119 | loop fusion | flops 39059456 | bytes 26839040 | tf_op jit(solution)/shard_map/convert_element_type | solution.py:375
  139.7 2.0 %collective-permute-start.21 = (bf16[2,16,2048]{2,1,0:T(8,128)(2,1)S(1)}, bf16[2,16,2048]{2,1,0:T(8,128)(2,1)S(1)}, u32[]{:S(2)}, u32[]{:S(2)}) collective-permute-start(bf16[2,16,2048]{2,1,0:T(8,128)(2,1)S(1)} %fusion.57), channel_id=1, source_target_pairs={{0,2},{1,3},{2,0},{3,1},{4,6},{5,7},{6,4},{7,5},{8,10},{9,11},{10,... | collective-permute-start | bytes 393224 | tf_op jit(solution)/shard_map/ppermute | solution.py:45
  142.2 7.7 %fusion.51 = bf16[16,32,512]{2,1,0:T(8,128)(2,1)S(1)} fusion(bf16[1,32,32,512]{3,2,1,0:T(8,128)(2,1)S(1)} %copy-done.1, bf16[38,38,512]{2,1,0:T(8,128)(2,1)S(1)} %copy-done.9, f32[512]{0:T(512)S(1)} %bitcast.427, f32[512]{0:T(512)S(1)} %bitcast.431, f32[512]{0:T(512)S(1)} %bitcast.243, f32[512]{0:T(512)S(1)} %bitcast.247, f32[512]{0:T(512)S(1)} %bitcast.251, ...), kind=kLoop, calls=%fused_computation.117 | loop fusion | flops 39059456 | bytes 26839040 | tf_op jit(solution)/shard_map/convert_element_type | solution.py:375
  150.4 4.5 %collective-permute-start.24 = (bf16[16,2048]{1,0:T(8,128)(2,1)S(1)}, bf16[16,2048]{1,0:T(8,128)(2,1)S(1)}, u32[]{:S(2)}, u32[]{:S(2)}) collective-permute-start(bf16[16,2048]{1,0:T(8,128)(2,1)S(1)} %fusion.59), channel_id=1, source_target_pairs={{0,4},{1,5},{2,6},{3,7},{4,0},{5,1},{6,2},{7,3},{8,12},{9,13},{10,... | collective-permute-start | bytes 196616 | tf_op jit(solution)/shard_map/ppermute | solution.py:45
  156.0 2.9 %collective-permute-done.24 = bf16[16,2048]{1,0:T(8,128)(2,1)S(1)} collective-permute-done((bf16[16,2048]{1,0:T(8,128)(2,1)S(1)}, bf16[16,2048]{1,0:T(8,128)(2,1)S(1)}, u32[]{:S(2)}, u32[]{:S(2)}) %collective-permute-start.24) | collective-permute-done | bytes 65568 | tf_op jit(solution)/shard_map/ppermute | solution.py:45
  161.3 4.3 %collective-permute-done.27 = f32[58,512]{1,0:T(8,128)S(1)} collective-permute-done((f32[58,512]{1,0:T(8,128)S(1)}, f32[58,512]{1,0:T(8,128)S(1)}, u32[]{:S(2)}, u32[]{:S(2)}) %collective-permute-start.27) | collective-permute-done | bytes 118816 | tf_op jit(solution)/shard_map/ppermute | solution.py:45
  167.5 5.6 %collective-permute-done.28 = f32[58,512]{1,0:T(8,128)S(1)} collective-permute-done((f32[58,512]{1,0:T(8,128)S(1)}, f32[58,512]{1,0:T(8,128)S(1)}, u32[]{:S(2)}, u32[]{:S(2)}) %collective-permute-start.28) | collective-permute-done | bytes 118816 | tf_op jit(solution)/shard_map/ppermute | solution.py:45
  (263 shorter events, 51.1 us)
Async XLA Ops:
  0.7 13.8 %collective-permute-start.3 = (bf16[64,512]{1,0:T(8,128)(2,1)}, bf16[64,512]{1,0:T(8,128)(2,1)S(1)}, u32[]{:S(2)}, u32[]{:S(2)}) collective-permute-start(bf16[64,512]{1,0:T(8,128)(2,1)} %param.19), channel_id=1, source_target_pairs={{0,4},{1,5},{2,6},{3,7},{4,0},{5,1},{6,2},{7,3},{8,12},{9,13},{10,... | collective-permute-start | bytes 196616 | tf_op jit(solution)/shard_map/ppermute | solution.py:45
  4.8 14.2 %collective-permute-start = (bf16[16,2048]{1,0:T(8,128)(2,1)}, bf16[16,2048]{1,0:T(8,128)(2,1)S(1)}, u32[]{:S(2)}, u32[]{:S(2)}) collective-permute-start(bf16[16,2048]{1,0:T(8,128)(2,1)} %param.17), channel_id=1, source_target_pairs={{0,4},{1,5},{2,6},{3,7},{4,0},{5,1},{6,2},{7,3},{8,12},{9,13},{10,... | collective-permute-start | bytes 196616 | tf_op jit(solution)/shard_map/ppermute | solution.py:45
  6.0 14.0 %collective-permute-start.6 = (bf16[32,3,512]{2,1,0:T(4,128)(2,1)S(1)}, bf16[32,3,512]{2,1,0:T(4,128)(2,1)S(1)}, u32[]{:S(2)}, u32[]{:S(2)}) collective-permute-start(bf16[32,3,512]{2,1,0:T(4,128)(2,1)S(1)} %get-tuple-element.284), channel_id=1, source_target_pairs={{0,1},{1,2},{2,3},{3,4},{4,5},{5,6},{6,7},{8,9},{9,10},{10,11},{11... | collective-permute-start | bytes 294920 | tf_op jit(solution)/shard_map/ppermute | solution.py:21
  9.7 10.3 %collective-permute-start.7 = (bf16[32,3,512]{2,1,0:T(4,128)(2,1)S(1)}, bf16[32,3,512]{2,1,0:T(4,128)(2,1)S(1)}, u32[]{:S(2)}, u32[]{:S(2)}) collective-permute-start(bf16[32,3,512]{2,1,0:T(4,128)(2,1)S(1)} %get-tuple-element.285), channel_id=1, source_target_pairs={{1,0},{2,1},{3,2},{4,3},{5,4},{6,5},{7,6},{9,8},{10,9},{11,10},{12... | collective-permute-start | bytes 294920 | tf_op jit(solution)/shard_map/ppermute | solution.py:22
  15.3 7.6 %collective-permute-start.4 = (bf16[2,64,512]{2,1,0:T(8,128)(2,1)S(1)}, bf16[2,64,512]{2,1,0:T(8,128)(2,1)S(1)}, u32[]{:S(2)}, u32[]{:S(2)}) collective-permute-start(bf16[2,64,512]{2,1,0:T(8,128)(2,1)S(1)} %pad_maximum_fusion.10), channel_id=1, source_target_pairs={{0,2},{1,3},{2,0},{3,1},{4,6},{5,7},{6,4},{7,5},{8,10},{9,11},{10,... | collective-permute-start | bytes 393224 | tf_op jit(solution)/shard_map/ppermute | solution.py:45
  31.6 11.2 %collective-permute-start.8 = (bf16[2,2,2,16,2048]{4,3,0,1,2:T(8,128)(2,1)S(1)}, bf16[2,2,2,16,2048]{4,3,0,1,2:T(8,128)(2,1)S(1)}, u32[]{:S(2)}, u32[]{:S(2)}) collective-permute-start(bf16[2,2,2,16,2048]{4,3,0,1,2:T(8,128)(2,1)S(1)} %pad_maximum_fusion.5), channel_id=1, source_target_pairs={{0,16},{8,24},{16,0},{24,8},{1,17},{9,25},{17,1},{25,9},{2,18},{10... | collective-permute-start | bytes 1572872 | tf_op jit(solution)/shard_map/ppermute | solution.py:45
  33.2 11.0 %collective-permute-start.9 = (bf16[2,2,2,64,512]{4,3,1,2,0:T(8,128)(2,1)S(1)}, bf16[2,2,2,64,512]{4,3,1,2,0:T(8,128)(2,1)S(1)}, u32[]{:S(2)}, u32[]{:S(2)}) collective-permute-start(bf16[2,2,2,64,512]{4,3,1,2,0:T(8,128)(2,1)S(1)} %pad_maximum_fusion.6), channel_id=1, source_target_pairs={{0,1},{1,0},{2,3},{3,2},{4,5},{5,4},{6,7},{7,6},{8,9},{9,8},{10,11... | collective-permute-start | bytes 1572872 | tf_op jit(solution)/shard_map/ppermute | solution.py:45
  44.5 8.5 %collective-permute-start.10 = (bf16[2,2,2,2,16,2048]{5,4,1,2,3,0:T(8,128)(2,1)S(1)}, bf16[2,2,2,2,16,2048]{5,4,1,2,3,0:T(8,128)(2,1)S(1)}, u32[]{:S(2)}, u32[]{:S(2)}) collective-permute-start(bf16[2,2,2,2,16,2048]{5,4,1,2,3,0:T(8,128)(2,1)S(1)} %pad_maximum_fusion.2), channel_id=1, source_target_pairs={{0,8},{8,0},{16,24},{24,16},{1,9},{9,1},{17,25},{25,17},{2,10},{10... | collective-permute-start | bytes 3145736 | tf_op jit(solution)/shard_map/ppermute | solution.py:45
  44.6 8.4 %collective-permute-start.11 = (bf16[2,2,2,2,64,512]{5,4,1,2,0,3:T(8,128)(2,1)S(1)}, bf16[2,2,2,2,64,512]{5,4,1,2,0,3:T(8,128)(2,1)S(1)}, u32[]{:S(2)}, u32[]{:S(2)}) collective-permute-start(bf16[2,2,2,2,64,512]{5,4,1,2,0,3:T(8,128)(2,1)S(1)} %pad_maximum_fusion.3), channel_id=1, source_target_pairs={{0,8},{8,0},{16,24},{24,16},{1,9},{9,1},{17,25},{25,17},{2,10},{10... | collective-permute-start | bytes 3145736 | tf_op jit(solution)/shard_map/ppermute | solution.py:45
  80.0 20.2 %collective-permute-start.16 = (bf16[32,3,512]{2,1,0:T(4,128)(2,1)}, bf16[32,3,512]{2,1,0:T(4,128)(2,1)S(1)}, u32[]{:S(2)}, u32[]{:S(2)}) collective-permute-start(bf16[32,3,512]{2,1,0:T(4,128)(2,1)} %get-tuple-element.278), channel_id=1, source_target_pairs={{0,1},{1,2},{2,3},{3,4},{4,5},{5,6},{6,7},{8,9},{9,10},{10,11},{11... | collective-permute-start | bytes 294920 | tf_op jit(solution)/shard_map/ppermute | solution.py:21
  83.7 16.6 %collective-permute-start.17 = (bf16[32,3,512]{2,1,0:T(4,128)(2,1)}, bf16[32,3,512]{2,1,0:T(4,128)(2,1)S(1)}, u32[]{:S(2)}, u32[]{:S(2)}) collective-permute-start(bf16[32,3,512]{2,1,0:T(4,128)(2,1)} %get-tuple-element.279), channel_id=1, source_target_pairs={{1,0},{2,1},{3,2},{4,3},{5,4},{6,5},{7,6},{9,8},{10,9},{11,10},{12... | collective-permute-start | bytes 294920 | tf_op jit(solution)/shard_map/ppermute | solution.py:22
  92.1 10.1 %collective-permute-start.12 = (bf16[2,2,2,2,16,2048]{5,4,1,2,3,0:T(8,128)(2,1)}, bf16[2,2,2,2,16,2048]{5,4,1,2,3,0:T(8,128)(2,1)}, u32[]{:S(2)}, u32[]{:S(2)}) collective-permute-start(bf16[2,2,2,2,16,2048]{5,4,1,2,3,0:T(8,128)(2,1)} %bitcast.216), channel_id=1, source_target_pairs={{0,8},{8,0},{16,24},{24,16},{1,9},{9,1},{17,25},{25,17},{2,10},{10... | collective-permute-start | bytes 3145736 | tf_op jit(solution)/shard_map/ppermute | solution.py:45
  92.1 10.1 %collective-permute-start.13 = (bf16[2,2,2,2,64,512]{5,4,1,2,0,3:T(8,128)(2,1)}, bf16[2,2,2,2,64,512]{5,4,1,2,0,3:T(8,128)(2,1)}, u32[]{:S(2)}, u32[]{:S(2)}) collective-permute-start(bf16[2,2,2,2,64,512]{5,4,1,2,0,3:T(8,128)(2,1)} %bitcast.215), channel_id=1, source_target_pairs={{0,8},{8,0},{16,24},{24,16},{1,9},{9,1},{17,25},{25,17},{2,10},{10... | collective-permute-start | bytes 3145736 | tf_op jit(solution)/shard_map/ppermute | solution.py:45
  105.7 14.5 %collective-permute-start.14 = (bf16[2,2,2,16,2048]{4,3,0,1,2:T(8,128)(2,1)S(1)}, bf16[2,2,2,16,2048]{4,3,0,1,2:T(8,128)(2,1)S(1)}, u32[]{:S(2)}, u32[]{:S(2)}) collective-permute-start(bf16[2,2,2,16,2048]{4,3,0,1,2:T(8,128)(2,1)S(1)} %fusion.53), channel_id=1, source_target_pairs={{0,16},{8,24},{16,0},{24,8},{1,17},{9,25},{17,1},{25,9},{2,18},{10... | collective-permute-start | bytes 1572872 | tf_op jit(solution)/shard_map/ppermute | solution.py:45
  106.2 14.5 %collective-permute-start.15 = (bf16[2,2,2,64,512]{4,3,1,2,0:T(8,128)(2,1)S(1)}, bf16[2,2,2,64,512]{4,3,1,2,0:T(8,128)(2,1)S(1)}, u32[]{:S(2)}, u32[]{:S(2)}) collective-permute-start(bf16[2,2,2,64,512]{4,3,1,2,0:T(8,128)(2,1)S(1)} %fusion.54), channel_id=1, source_target_pairs={{0,1},{1,0},{2,3},{3,2},{4,5},{5,4},{6,7},{7,6},{8,9},{9,8},{10,11... | collective-permute-start | bytes 1572872 | tf_op jit(solution)/shard_map/ppermute | solution.py:45
  127.8 11.6 %collective-permute-start.18 = (bf16[2,2,16,2048]{3,2,0,1:T(8,128)(2,1)}, bf16[2,2,16,2048]{3,2,0,1:T(8,128)(2,1)S(1)}, u32[]{:S(2)}, u32[]{:S(2)}) collective-permute-start(bf16[2,2,16,2048]{3,2,0,1:T(8,128)(2,1)} %fusion.55), channel_id=1, source_target_pairs={{0,1},{1,0},{2,3},{3,2},{4,5},{5,4},{6,7},{7,6},{8,9},{9,8},{10,11... | collective-permute-start | bytes 786440 | tf_op jit(solution)/shard_map/ppermute | solution.py:45
  129.6 9.8 %collective-permute-start.19 = (bf16[2,2,64,512]{3,2,0,1:T(8,128)(2,1)}, bf16[2,2,64,512]{3,2,0,1:T(8,128)(2,1)S(1)}, u32[]{:S(2)}, u32[]{:S(2)}) collective-permute-start(bf16[2,2,64,512]{3,2,0,1:T(8,128)(2,1)} %fusion.56), channel_id=1, source_target_pairs={{0,16},{8,24},{16,0},{24,8},{1,17},{9,25},{17,1},{25,9},{2,18},{10... | collective-permute-start | bytes 786440 | tf_op jit(solution)/shard_map/ppermute | solution.py:45
  131.3 8.1 %collective-permute-start.20 = (f32[58,512]{1,0:T(8,128)S(1)}, f32[58,512]{1,0:T(8,128)S(1)}, u32[]{:S(2)}, u32[]{:S(2)}) collective-permute-start(f32[58,512]{1,0:T(8,128)S(1)} %concatenate.17), channel_id=1, source_target_pairs={{0,8},{8,0},{16,24},{24,16},{1,9},{9,1},{17,25},{25,17},{2,10},{10... | collective-permute-start | bytes 356360 | tf_op jit(solution)/shard_map/ppermute | solution.py:45
  139.7 10.2 %collective-permute-start.21 = (bf16[2,16,2048]{2,1,0:T(8,128)(2,1)S(1)}, bf16[2,16,2048]{2,1,0:T(8,128)(2,1)S(1)}, u32[]{:S(2)}, u32[]{:S(2)}) collective-permute-start(bf16[2,16,2048]{2,1,0:T(8,128)(2,1)S(1)} %fusion.57), channel_id=1, source_target_pairs={{0,2},{1,3},{2,0},{3,1},{4,6},{5,7},{6,4},{7,5},{8,10},{9,11},{10,... | collective-permute-start | bytes 393224 | tf_op jit(solution)/shard_map/ppermute | solution.py:45
  141.7 8.2 %collective-permute-start.22 = (bf16[2,64,512]{2,1,0:T(8,128)(2,1)S(1)}, bf16[2,64,512]{2,1,0:T(8,128)(2,1)S(1)}, u32[]{:S(2)}, u32[]{:S(2)}) collective-permute-start(bf16[2,64,512]{2,1,0:T(8,128)(2,1)S(1)} %fusion.58), channel_id=1, source_target_pairs={{0,2},{1,3},{2,0},{3,1},{4,6},{5,7},{6,4},{7,5},{8,10},{9,11},{10,... | collective-permute-start | bytes 393224 | tf_op jit(solution)/shard_map/ppermute | solution.py:45
  141.8 8.0 %collective-permute-start.23 = (f32[58,512]{1,0:T(8,128)S(1)}, f32[58,512]{1,0:T(8,128)S(1)}, u32[]{:S(2)}, u32[]{:S(2)}) collective-permute-start(f32[58,512]{1,0:T(8,128)S(1)} %add.902), channel_id=1, source_target_pairs={{0,16},{8,24},{16,0},{24,8},{1,17},{9,25},{17,1},{25,9},{2,18},{10... | collective-permute-start | bytes 356360 | tf_op jit(solution)/shard_map/ppermute | solution.py:45
  150.0 10.5 %collective-permute-start.26 = (f32[58,512]{1,0:T(8,128)S(1)}, f32[58,512]{1,0:T(8,128)S(1)}, u32[]{:S(2)}, u32[]{:S(2)}) collective-permute-start(f32[58,512]{1,0:T(8,128)S(1)} %add.956), channel_id=1, source_target_pairs={{0,1},{1,0},{2,3},{3,2},{4,5},{5,4},{6,7},{7,6},{8,9},{9,8},{10,11... | collective-permute-start | bytes 356360 | tf_op jit(solution)/shard_map/ppermute | solution.py:45
  150.4 8.5 %collective-permute-start.24 = (bf16[16,2048]{1,0:T(8,128)(2,1)S(1)}, bf16[16,2048]{1,0:T(8,128)(2,1)S(1)}, u32[]{:S(2)}, u32[]{:S(2)}) collective-permute-start(bf16[16,2048]{1,0:T(8,128)(2,1)S(1)} %fusion.59), channel_id=1, source_target_pairs={{0,4},{1,5},{2,6},{3,7},{4,0},{5,1},{6,2},{7,3},{8,12},{9,13},{10,... | collective-permute-start | bytes 196616 | tf_op jit(solution)/shard_map/ppermute | solution.py:45
  165.6 7.5 %collective-permute-start.28 = (f32[58,512]{1,0:T(8,128)S(1)}, f32[58,512]{1,0:T(8,128)S(1)}, u32[]{:S(2)}, u32[]{:S(2)}) collective-permute-start(f32[58,512]{1,0:T(8,128)S(1)} %add.958), channel_id=1, source_target_pairs={{0,4},{1,5},{2,6},{3,7},{4,0},{5,1},{6,2},{7,3},{8,12},{9,13},{10,... | collective-permute-start | bytes 356360 | tf_op jit(solution)/shard_map/ppermute | solution.py:45
  (82 other events, 1063.7 us)

commit v4 on v3

--- a/solution.py
+++ b/solution.py
@@ -365,7 +365,11 @@
         else:
             first_sent, second_sent, small, p = tied(first_sent, second_sent, small, grad_padded)
             first_got, second_got = swapped(first_sent, in_key), swapped(second_sent, out_key)
-            small_got = swapped(small, small_keys.pop(0))
+            group = [small_keys.pop(0)]
+            if k < 4 and small_keys and small_keys[0][0] == group[0][0]:
+                axis, stride = small_keys.pop(0)
+                group += [(axis, stride), (axis, stride + group[0][1])]
+            small_got = tuple(swapped(small, key) for key in group)
             result = ()
             if k < 4:
                 start = (k - 2) * half
@@ -376,7 +380,9 @@
             first_got, second_got, small_got, result = tied(
                 first_got, second_got, small_got, result
             )
-            small = small + small_got
+            small = small + small_got[0]
+            if len(group) == 3:
+                small = small + (small_got[1] + small_got[2])
             if k < 4:
                 back.append(result)
         first = first_kept + first_got.astype(jnp.float32)

time: 176 us -> 176 us (level)
  waiting for transfers between devices: 24.6 us -> 19.4 us
  starting transfers between devices: 40 us -> 44.9 us
    ppermute x25 -> x27, waiting for transfers between devices: 24.6 us -> 19.4 us  [swapped(): lax.ppermute(x, axis, [(i, i ^ stride) for i in range(lax.axis_size(axis))])]
    ppermute x25 -> x27, starting transfers between devices: 29.9 us -> 34.8 us  [swapped(): lax.ppermute(x, axis, [(i, i ^ stride) for i in range(lax.axis_size(axis))])]
  transfers between devices with their start and end apart: 29 -> 31, of which waited for: 11 -> 12; matrix products, arithmetic and copies ran while one was open for 38% -> 38% of each run, Pallas kernels for 0% -> 0%
where the time goes in v4:
time: 176 us; the launch traced here: 175 us
  other arithmetic  60.3 us (34%)
  starting transfers between devices  44.9 us (26%)
  local copies, waits for them, and re-layouts  26.6 us (15%)
  Pallas kernels  21.2 us (12%)
  waiting for transfers between devices  19.4 us (11%)
  between operations  2.28 us (1%)
    ppermute x27, starting transfers between devices, swapped(): lax.ppermute(x, axis, [(i, i ^ stride) for i in range(lax.axis_size(axis))])  34.8 us
    pallas_call x1, Pallas kernels, norm_mlp(): pl.pallas_call(norm_mlp_kernel, grid=(units // tile,), in_specs=[whole, w...  21.2 us
    ppermute x27, waiting for transfers between devices, swapped(): lax.ppermute(x, axis, [(i, i ^ stride) for i in range(lax.axis_size(axis))])  19.4 us
    reduce_sum x3, other arithmetic, kernel_gradient(): taps.append(jnp.sum(grad_wide * window, axis=(0, 1)))  16.1 us
    convert_element_type x2, other arithmetic, local(): result = wide.astype(jnp.bfloat16)  15.6 us
    convert_element_type x2, other arithmetic, conv_forward(): return (summed + offset).astype(jnp.bfloat16)  15.3 us
    ppermute x2, starting transfers between devices, padded_2(): before = lax.ppermute(last, axis, up)  7.32 us
    concatenate x1, local copies, waits for them, and re-layouts, local(): jnp.concatenate([jnp.stack(taps)] + [part.reshape(-1, channels) for part...  4.45 us
  transfers between devices with their start and end apart: 31, of which 12 were waited for; matrix products, arithmetic and copies ran while one was open for 38% of the time, Pallas kernels for 0%

profile of v4, /device:TPU:0, one launch (start us, length us, event | category | flops | bytes accessed | tf_op | source)
XLA Modules:
  0.0 174.8 jit_solution(16519203353752654007)
XLA Ops:
  0.7 4.1 %collective-permute-start.3 = (bf16[64,512]{1,0:T(8,128)(2,1)}, bf16[64,512]{1,0:T(8,128)(2,1)S(1)}, u32[]{:S(2)}, u32[]{:S(2)}) collective-permute-start(bf16[64,512]{1,0:T(8,128)(2,1)} %param.19), channel_id=1, source_target_pairs={{0,4},{1,5},{2,6},{3,7},{4,0},{5,1},{6,2},{7,3},{8,12},{9,13},{10,... | collective-permute-start | bytes 196616 | tf_op jit(solution)/shard_map/ppermute | solution.py:45
  6.0 3.7 %collective-permute-start.6 = (bf16[32,3,512]{2,1,0:T(4,128)(2,1)S(1)}, bf16[32,3,512]{2,1,0:T(4,128)(2,1)S(1)}, u32[]{:S(2)}, u32[]{:S(2)}) collective-permute-start(bf16[32,3,512]{2,1,0:T(4,128)(2,1)S(1)} %get-tuple-element.292), channel_id=1, source_target_pairs={{0,1},{1,2},{2,3},{3,4},{4,5},{5,6},{6,7},{8,9},{9,10},{10,11},{11... | collective-permute-start | bytes 294920 | tf_op jit(solution)/shard_map/ppermute | solution.py:21
  15.3 3.7 %collective-permute-start.4 = (bf16[2,64,512]{2,1,0:T(8,128)(2,1)S(1)}, bf16[2,64,512]{2,1,0:T(8,128)(2,1)S(1)}, u32[]{:S(2)}, u32[]{:S(2)}) collective-permute-start(bf16[2,64,512]{2,1,0:T(8,128)(2,1)S(1)} %pad_maximum_fusion.10), channel_id=1, source_target_pairs={{0,2},{1,3},{2,0},{3,1},{4,6},{5,7},{6,4},{7,5},{8,10},{9,11},{10,... | collective-permute-start | bytes 393224 | tf_op jit(solution)/shard_map/ppermute | solution.py:45
  20.8 2.2 %collective-permute-done.4 = bf16[2,64,512]{2,1,0:T(8,128)(2,1)S(1)} collective-permute-done((bf16[2,64,512]{2,1,0:T(8,128)(2,1)S(1)}, bf16[2,64,512]{2,1,0:T(8,128)(2,1)S(1)}, u32[]{:S(2)}, u32[]{:S(2)}) %collective-permute-start.4) | collective-permute-done | bytes 131104 | tf_op jit(solution)/shard_map/ppermute | solution.py:45
  26.2 3.3 %collective-permute-done.5 = bf16[2,2,64,512]{3,2,0,1:T(8,128)(2,1)S(1)} collective-permute-done((bf16[2,2,64,512]{3,2,0,1:T(8,128)(2,1)S(1)}, bf16[2,2,64,512]{3,2,0,1:T(8,128)(2,1)S(1)}, u32[]{:S(2)}, u32[]{:S(2)}) %collective-permute-start.5) | collective-permute-done | bytes 262176 | tf_op jit(solution)/shard_map/ppermute | solution.py:45
  29.6 2.0 %collective-permute-done.2 = bf16[2,2,16,2048]{3,2,0,1:T(8,128)(2,1)S(1)} collective-permute-done((bf16[2,2,16,2048]{3,2,0,1:T(8,128)(2,1)S(1)}, bf16[2,2,16,2048]{3,2,0,1:T(8,128)(2,1)S(1)}, u32[]{:S(2)}, u32[]{:S(2)}) %collective-permute-start.2) | collective-permute-done | bytes 262176 | tf_op jit(solution)/shard_map/ppermute | solution.py:45
  34.5 7.6 %add_convert_fusion.1 = bf16[16,32,512]{2,1,0:T(8,128)(2,1)S(1)} fusion(f32[512]{0:T(512)S(1)} %copy-done.58, bf16[38,38,512]{2,1,0:T(8,128)(2,1)S(1)} %select_maximum_fusion.2, f32[512]{0:T(512)S(1)} %bitcast.424, f32[512]{0:T(512)S(1)} %bitcast.428, f32[512]{0:T(512)S(1)} %bitcast.240, f32[512]{0:T(512)S(1)} %bitcast.244, f32[512]{0:T(512)S(1)} %bitcast.248, ...), kind=kLoop, calls=%fused_computation.131 | loop fusion | flops 38797312 | bytes 26316800 | tf_op jit(solution)/shard_map/convert_element_type | solution.py:100
  45.3 7.7 %add_convert_fusion = bf16[16,32,512]{2,1,0:T(8,128)(2,1)S(1)} fusion(bf16[38,38,512]{2,1,0:T(8,128)(2,1)S(1)} %select_maximum_fusion.2, f32[512]{0:T(512)S(1)} %copy-done.58, f32[512]{0:T(512)S(1)} %bitcast.425, f32[512]{0:T(512)S(1)} %bitcast.429, f32[512]{0:T(512)S(1)} %bitcast.241, f32[512]{0:T(512)S(1)} %bitcast.245, f32[512]{0:T(512)S(1)} %bitcast.249, ...), kind=kLoop, calls=%fused_computation.130 | loop fusion | flops 38797312 | bytes 26316800 | tf_op jit(solution)/shard_map/convert_element_type | solution.py:100
  58.0 21.2 %shard_map.194 = (bf16[1024,512]{1,0:T(8,128)(2,1)}, bf16[1024,512]{1,0:T(8,128)(2,1)S(1)}, f32[1,512]{1,0:T(1,128)S(1)}, f32[1,512]{1,0:T(1,128)S(1)}, bf16[512...) custom-call(bf16[1024,512]{1,0:T(8,128)(2,1)S(1)} %bitcast.226, ...), custom_call_target="tpu_custom_call" | custom-call | flops 12884901888 | bytes 16777216 | tf_op jit(solution)/shard_map/pallas_call | solution.py:238
  80.0 3.6 %collective-permute-start.16 = (bf16[32,3,512]{2,1,0:T(4,128)(2,1)}, bf16[32,3,512]{2,1,0:T(4,128)(2,1)S(1)}, u32[]{:S(2)}, u32[]{:S(2)}) collective-permute-start(bf16[32,3,512]{2,1,0:T(4,128)(2,1)} %get-tuple-element.286), channel_id=1, source_target_pairs={{0,1},{1,2},{2,3},{3,4},{4,5},{5,6},{6,7},{8,9},{9,10},{10,11},{11... | collective-permute-start | bytes 294920 | tf_op jit(solution)/shard_map/ppermute | solution.py:21
  85.2 2.7 %constant_dynamic-slice_fusion = (bf16[2,1,2,2,2,64,512]{6,5,4,3,2,1,0:T(8,128)(2,1)}, bf16[2,1,2,2,2,64,512]{6,5,4,3,2,1,0:T(8,128)(2,1)S(1)}) fusion(bf16[2,2,2,2,2,64,512]{6,5,4,3,2,1,0:T(8,128)(2,1)} %bitcast.233, s32[]{:T(128)S(6)} %select_n.288, s32[]{:T(128)S(6)} %select_n.289), kind=kLoop, calls=%fused_computation.177 | loop fusion | bytes 4194312 | tf_op jit(solution)/shard_map/jit(dynamic_index_in_dim)/dynamic_slice | solution.py:65
  92.6 4.6 %fusion.14 = (f32[512]{0:T(512)}, f32[512]{0:T(512)}, f32[512]{0:T(512)}, f32[512]{0:T(512)}, f32[512]{0:T(512)}, /*index=5*/f32[512]{0:T(512)}, f32[512]{0:T(51...) fusion(bf16[32,32,512]{2,1,0:T(8,128)(2,1)S(1)} %bitcast.218, ...), kind=kLoop, calls=%fused_computation.65 | loop fusion | flops 22537216 | bytes 15757312 | tf_op jit(solution)/shard_map/reduce_sum | solution.py:124
  100.3 1.9 %select_maximum_fusion = bf16[38,38,512]{2,1,0:T(8,128)(2,1)} fusion(bf16[32,3,512]{2,1,0:T(4,128)(2,1)S(1)} %collective-permute-done.17, bf16[32,32,512]{2,1,0:T(8,128)(2,1)S(1)} %bitcast.219, bf16[32,3,512]{2,1,0:T(4,128)(2,1)S(1)} %collective-permute-done.16), kind=kLoop, calls=%fused_computation.105 | loop fusion | flops 8871936 | bytes 2723840 | tf_op jit(solution)/shard_map/concatenate | solution.py:23
  106.2 2.6 %collective-permute-start.15 = (bf16[2,2,2,64,512]{4,3,1,2,0:T(8,128)(2,1)S(1)}, bf16[2,2,2,64,512]{4,3,1,2,0:T(8,128)(2,1)S(1)}, u32[]{:S(2)}, u32[]{:S(2)}) collective-permute-start(bf16[2,2,2,64,512]{4,3,1,2,0:T(8,128)(2,1)S(1)} %fusion.54), channel_id=1, source_target_pairs={{0,1},{1,0},{2,3},{3,2},{4,5},{5,4},{6,7},{7,6},{8,9},{9,8},{10,11... | collective-permute-start | bytes 1572872 | tf_op jit(solution)/shard_map/ppermute | solution.py:45
  108.8 6.0 %fusion.49 = (f32[512]{0:T(512)}, f32[512]{0:T(512)}, f32[512]{0:T(512)}, f32[512]{0:T(512)}, f32[512]{0:T(512)}, /*index=5*/f32[512]{0:T(512)}, f32[512]{0:T(51...) fusion(bf16[32,32,512]{2,1,0:T(8,128)(2,1)S(1)} %bitcast.220, ...), kind=kLoop, calls=%fused_computation.100 | loop fusion | flops 28826624 | bytes 19959808 | tf_op jit(solution)/shard_map/reduce_sum | solution.py:124
  114.8 5.5 %fusion.48 = (f32[512]{0:T(512)S(1)}, f32[512]{0:T(512)S(1)}, f32[512]{0:T(512)}, f32[512]{0:T(512)}, f32[512]{0:T(512)}, /*index=5*/f32[512]{0:T(512)}, f32[512...) fusion(bf16[32,32,512]{2,1,0:T(8,128)(2,1)S(1)} %bitcast.221, ...), kind=kLoop, calls=%fused_computation.99 | loop fusion | flops 27254272 | bytes 18909184 | tf_op jit(solution)/shard_map/reduce_sum | solution.py:124
  123.3 4.5 %concatenate.17 = f32[58,512]{1,0:T(8,128)S(1)} concatenate(f32[1,512]{1,0:T(1,128)S(1)} %bitcast.445, f32[1,512]{1,0:T(1,128)S(1)} %bitcast.433, f32[1,512]{1,0:T(1,128)S(1)} %bitcast.434, f32[1,512]{1,0:T(1,128)S(1)} %bitcast.435, f32[1,512]{1,0:T(1,128)S(1)} %bitcast.436, f32[1,512]{1,0:T(1,128)S(1)} %bitcast.437, f32[1,512]{1,0:T(1,128)S(1)} %bitcast.438, ...), dimensions={0} | concatenate | bytes 237568 | tf_op jit(solution)/shard_map/concatenate | solution.py:362
  133.3 7.9 %fusion.52 = bf16[16,32,512]{2,1,0:T(8,128)(2,1)S(1)} fusion(bf16[1,32,32,512]{3,2,1,0:T(8,128)(2,1)S(1)} %copy-done.1, bf16[38,38,512]{2,1,0:T(8,128)(2,1)S(1)} %copy-done.9, f32[512]{0:T(512)S(1)} %bitcast.426, f32[512]{0:T(512)S(1)} %bitcast.430, f32[512]{0:T(512)S(1)} %bitcast.242, f32[512]{0:T(512)S(1)} %bitcast.246, f32[512]{0:T(512)S(1)} %bitcast.250, ...), kind=kLoop, calls=%fused_computation.119 | loop fusion | flops 39059456 | bytes 26839040 | tf_op jit(solution)/shard_map/convert_element_type | solution.py:379
  142.5 1.8 %collective-permute-start.25 = (f32[58,512]{1,0:T(8,128)S(1)}, f32[58,512]{1,0:T(8,128)S(1)}, u32[]{:S(2)}, u32[]{:S(2)}) collective-permute-start(f32[58,512]{1,0:T(8,128)S(1)} %add_add_fusion.1), channel_id=1, source_target_pairs={{0,1},{1,0},{2,3},{3,2},{4,5},{5,4},{6,7},{7,6},{8,9},{9,8},{10,11... | collective-permute-start | bytes 356360 | tf_op jit(solution)/shard_map/ppermute | solution.py:45
  144.3 1.9 %collective-permute-start.26 = (f32[58,512]{1,0:T(8,128)S(1)}, f32[58,512]{1,0:T(8,128)S(1)}, u32[]{:S(2)}, u32[]{:S(2)}) collective-permute-start(f32[58,512]{1,0:T(8,128)S(1)} %add_add_fusion.1), channel_id=1, source_target_pairs={{0,2},{1,3},{2,0},{3,1},{4,6},{5,7},{6,4},{7,5},{8,10},{9,11},{10,... | collective-permute-start | bytes 356360 | tf_op jit(solution)/shard_map/ppermute | solution.py:45
  148.3 7.7 %fusion.51 = bf16[16,32,512]{2,1,0:T(8,128)(2,1)S(1)} fusion(bf16[1,32,32,512]{3,2,1,0:T(8,128)(2,1)S(1)} %copy-done.1, bf16[38,38,512]{2,1,0:T(8,128)(2,1)S(1)} %copy-done.9, f32[512]{0:T(512)S(1)} %bitcast.427, f32[512]{0:T(512)S(1)} %bitcast.431, f32[512]{0:T(512)S(1)} %bitcast.243, f32[512]{0:T(512)S(1)} %bitcast.247, f32[512]{0:T(512)S(1)} %bitcast.251, ...), kind=kLoop, calls=%fused_computation.117 | loop fusion | flops 39059456 | bytes 26839040 | tf_op jit(solution)/shard_map/convert_element_type | solution.py:379
  157.8 3.1 %collective-permute-start.30 = (f32[58,512]{1,0:T(8,128)S(1)}, f32[58,512]{1,0:T(8,128)S(1)}, u32[]{:S(2)}, u32[]{:S(2)}) collective-permute-start(f32[58,512]{1,0:T(8,128)S(1)} %add_add_fusion), channel_id=1, source_target_pairs={{0,4},{1,5},{2,6},{3,7},{4,0},{5,1},{6,2},{7,3},{8,12},{9,13},{10,... | collective-permute-start | bytes 356360 | tf_op jit(solution)/shard_map/ppermute | solution.py:45
  161.0 2.8 %collective-permute-start.29 = (bf16[64,512]{1,0:T(8,128)(2,1)S(1)}, bf16[64,512]{1,0:T(8,128)(2,1)S(1)}, u32[]{:S(2)}, u32[]{:S(2)}) collective-permute-start(bf16[64,512]{1,0:T(8,128)(2,1)S(1)} %fusion.60), channel_id=1, source_target_pairs={{0,4},{1,5},{2,6},{3,7},{4,0},{5,1},{6,2},{7,3},{8,12},{9,13},{10,... | collective-permute-start | bytes 196616 | tf_op jit(solution)/shard_map/ppermute | solution.py:45
  164.9 5.9 %collective-permute-done.28 = bf16[16,2048]{1,0:T(8,128)(2,1)S(1)} collective-permute-done((bf16[16,2048]{1,0:T(8,128)(2,1)S(1)}, bf16[16,2048]{1,0:T(8,128)(2,1)S(1)}, u32[]{:S(2)}, u32[]{:S(2)}) %collective-permute-start.28) | collective-permute-done | bytes 65568 | tf_op jit(solution)/shard_map/ppermute | solution.py:45
  (265 shorter events, 54.5 us)
Async XLA Ops:
  0.7 13.8 %collective-permute-start.3 = (bf16[64,512]{1,0:T(8,128)(2,1)}, bf16[64,512]{1,0:T(8,128)(2,1)S(1)}, u32[]{:S(2)}, u32[]{:S(2)}) collective-permute-start(bf16[64,512]{1,0:T(8,128)(2,1)} %param.19), channel_id=1, source_target_pairs={{0,4},{1,5},{2,6},{3,7},{4,0},{5,1},{6,2},{7,3},{8,12},{9,13},{10,... | collective-permute-start | bytes 196616 | tf_op jit(solution)/shard_map/ppermute | solution.py:45
  4.8 14.2 %collective-permute-start = (bf16[16,2048]{1,0:T(8,128)(2,1)}, bf16[16,2048]{1,0:T(8,128)(2,1)S(1)}, u32[]{:S(2)}, u32[]{:S(2)}) collective-permute-start(bf16[16,2048]{1,0:T(8,128)(2,1)} %param.17), channel_id=1, source_target_pairs={{0,4},{1,5},{2,6},{3,7},{4,0},{5,1},{6,2},{7,3},{8,12},{9,13},{10,... | collective-permute-start | bytes 196616 | tf_op jit(solution)/shard_map/ppermute | solution.py:45
  6.0 14.0 %collective-permute-start.6 = (bf16[32,3,512]{2,1,0:T(4,128)(2,1)S(1)}, bf16[32,3,512]{2,1,0:T(4,128)(2,1)S(1)}, u32[]{:S(2)}, u32[]{:S(2)}) collective-permute-start(bf16[32,3,512]{2,1,0:T(4,128)(2,1)S(1)} %get-tuple-element.292), channel_id=1, source_target_pairs={{0,1},{1,2},{2,3},{3,4},{4,5},{5,6},{6,7},{8,9},{9,10},{10,11},{11... | collective-permute-start | bytes 294920 | tf_op jit(solution)/shard_map/ppermute | solution.py:21
  9.7 10.3 %collective-permute-start.7 = (bf16[32,3,512]{2,1,0:T(4,128)(2,1)S(1)}, bf16[32,3,512]{2,1,0:T(4,128)(2,1)S(1)}, u32[]{:S(2)}, u32[]{:S(2)}) collective-permute-start(bf16[32,3,512]{2,1,0:T(4,128)(2,1)S(1)} %get-tuple-element.293), channel_id=1, source_target_pairs={{1,0},{2,1},{3,2},{4,3},{5,4},{6,5},{7,6},{9,8},{10,9},{11,10},{12... | collective-permute-start | bytes 294920 | tf_op jit(solution)/shard_map/ppermute | solution.py:22
  31.6 11.2 %collective-permute-start.8 = (bf16[2,2,2,16,2048]{4,3,0,1,2:T(8,128)(2,1)S(1)}, bf16[2,2,2,16,2048]{4,3,0,1,2:T(8,128)(2,1)S(1)}, u32[]{:S(2)}, u32[]{:S(2)}) collective-permute-start(bf16[2,2,2,16,2048]{4,3,0,1,2:T(8,128)(2,1)S(1)} %pad_maximum_fusion.5), channel_id=1, source_target_pairs={{0,16},{8,24},{16,0},{24,8},{1,17},{9,25},{17,1},{25,9},{2,18},{10... | collective-permute-start | bytes 1572872 | tf_op jit(solution)/shard_map/ppermute | solution.py:45
  33.2 11.0 %collective-permute-start.9 = (bf16[2,2,2,64,512]{4,3,1,2,0:T(8,128)(2,1)S(1)}, bf16[2,2,2,64,512]{4,3,1,2,0:T(8,128)(2,1)S(1)}, u32[]{:S(2)}, u32[]{:S(2)}) collective-permute-start(bf16[2,2,2,64,512]{4,3,1,2,0:T(8,128)(2,1)S(1)} %pad_maximum_fusion.6), channel_id=1, source_target_pairs={{0,1},{1,0},{2,3},{3,2},{4,5},{5,4},{6,7},{7,6},{8,9},{9,8},{10,11... | collective-permute-start | bytes 1572872 | tf_op jit(solution)/shard_map/ppermute | solution.py:45
  80.0 20.2 %collective-permute-start.16 = (bf16[32,3,512]{2,1,0:T(4,128)(2,1)}, bf16[32,3,512]{2,1,0:T(4,128)(2,1)S(1)}, u32[]{:S(2)}, u32[]{:S(2)}) collective-permute-start(bf16[32,3,512]{2,1,0:T(4,128)(2,1)} %get-tuple-element.286), channel_id=1, source_target_pairs={{0,1},{1,2},{2,3},{3,4},{4,5},{5,6},{6,7},{8,9},{9,10},{10,11},{11... | collective-permute-start | bytes 294920 | tf_op jit(solution)/shard_map/ppermute | solution.py:21
  83.7 16.6 %collective-permute-start.17 = (bf16[32,3,512]{2,1,0:T(4,128)(2,1)}, bf16[32,3,512]{2,1,0:T(4,128)(2,1)S(1)}, u32[]{:S(2)}, u32[]{:S(2)}) collective-permute-start(bf16[32,3,512]{2,1,0:T(4,128)(2,1)} %get-tuple-element.287), channel_id=1, source_target_pairs={{1,0},{2,1},{3,2},{4,3},{5,4},{6,5},{7,6},{9,8},{10,9},{11,10},{12... | collective-permute-start | bytes 294920 | tf_op jit(solution)/shard_map/ppermute | solution.py:22
  92.1 10.1 %collective-permute-start.12 = (bf16[2,2,2,2,16,2048]{5,4,1,2,3,0:T(8,128)(2,1)}, bf16[2,2,2,2,16,2048]{5,4,1,2,3,0:T(8,128)(2,1)}, u32[]{:S(2)}, u32[]{:S(2)}) collective-permute-start(bf16[2,2,2,2,16,2048]{5,4,1,2,3,0:T(8,128)(2,1)} %bitcast.216), channel_id=1, source_target_pairs={{0,8},{8,0},{16,24},{24,16},{1,9},{9,1},{17,25},{25,17},{2,10},{10... | collective-permute-start | bytes 3145736 | tf_op jit(solution)/shard_map/ppermute | solution.py:45
  92.1 10.1 %collective-permute-start.13 = (bf16[2,2,2,2,64,512]{5,4,1,2,0,3:T(8,128)(2,1)}, bf16[2,2,2,2,64,512]{5,4,1,2,0,3:T(8,128)(2,1)}, u32[]{:S(2)}, u32[]{:S(2)}) collective-permute-start(bf16[2,2,2,2,64,512]{5,4,1,2,0,3:T(8,128)(2,1)} %bitcast.215), channel_id=1, source_target_pairs={{0,8},{8,0},{16,24},{24,16},{1,9},{9,1},{17,25},{25,17},{2,10},{10... | collective-permute-start | bytes 3145736 | tf_op jit(solution)/shard_map/ppermute | solution.py:45
  105.7 14.5 %collective-permute-start.14 = (bf16[2,2,2,16,2048]{4,3,0,1,2:T(8,128)(2,1)S(1)}, bf16[2,2,2,16,2048]{4,3,0,1,2:T(8,128)(2,1)S(1)}, u32[]{:S(2)}, u32[]{:S(2)}) collective-permute-start(bf16[2,2,2,16,2048]{4,3,0,1,2:T(8,128)(2,1)S(1)} %fusion.53), channel_id=1, source_target_pairs={{0,16},{8,24},{16,0},{24,8},{1,17},{9,25},{17,1},{25,9},{2,18},{10... | collective-permute-start | bytes 1572872 | tf_op jit(solution)/shard_map/ppermute | solution.py:45
  106.2 14.5 %collective-permute-start.15 = (bf16[2,2,2,64,512]{4,3,1,2,0:T(8,128)(2,1)S(1)}, bf16[2,2,2,64,512]{4,3,1,2,0:T(8,128)(2,1)S(1)}, u32[]{:S(2)}, u32[]{:S(2)}) collective-permute-start(bf16[2,2,2,64,512]{4,3,1,2,0:T(8,128)(2,1)S(1)} %fusion.54), channel_id=1, source_target_pairs={{0,1},{1,0},{2,3},{3,2},{4,5},{5,4},{6,7},{7,6},{8,9},{9,8},{10,11... | collective-permute-start | bytes 1572872 | tf_op jit(solution)/shard_map/ppermute | solution.py:45
  127.8 13.5 %collective-permute-start.20 = (f32[58,512]{1,0:T(8,128)S(1)}, f32[58,512]{1,0:T(8,128)S(1)}, u32[]{:S(2)}, u32[]{:S(2)}) collective-permute-start(f32[58,512]{1,0:T(8,128)S(1)} %concatenate.17), channel_id=1, source_target_pairs={{0,8},{8,0},{16,24},{24,16},{1,9},{9,1},{17,25},{25,17},{2,10},{10... | collective-permute-start | bytes 356360 | tf_op jit(solution)/shard_map/ppermute | solution.py:45
  127.9 13.4 %collective-permute-start.21 = (f32[58,512]{1,0:T(8,128)S(1)}, f32[58,512]{1,0:T(8,128)S(1)}, u32[]{:S(2)}, u32[]{:S(2)}) collective-permute-start(f32[58,512]{1,0:T(8,128)S(1)} %concatenate.17), channel_id=1, source_target_pairs={{0,16},{8,24},{16,0},{24,8},{1,17},{9,25},{17,1},{25,9},{2,18},{10... | collective-permute-start | bytes 356360 | tf_op jit(solution)/shard_map/ppermute | solution.py:45
  129.6 11.7 %collective-permute-start.22 = (f32[58,512]{1,0:T(8,128)S(1)}, f32[58,512]{1,0:T(8,128)S(1)}, u32[]{:S(2)}, u32[]{:S(2)}) collective-permute-start(f32[58,512]{1,0:T(8,128)S(1)} %concatenate.17), channel_id=1, source_target_pairs={{0,24},{8,16},{16,8},{24,0},{1,25},{9,17},{17,9},{25,1},{2,26},{10... | collective-permute-start | bytes 356360 | tf_op jit(solution)/shard_map/ppermute | solution.py:45
  129.8 11.5 %collective-permute-start.18 = (bf16[2,2,16,2048]{3,2,0,1:T(8,128)(2,1)}, bf16[2,2,16,2048]{3,2,0,1:T(8,128)(2,1)S(1)}, u32[]{:S(2)}, u32[]{:S(2)}) collective-permute-start(bf16[2,2,16,2048]{3,2,0,1:T(8,128)(2,1)} %fusion.55), channel_id=1, source_target_pairs={{0,1},{1,0},{2,3},{3,2},{4,5},{5,4},{6,7},{7,6},{8,9},{9,8},{10,11... | collective-permute-start | bytes 786440 | tf_op jit(solution)/shard_map/ppermute | solution.py:45
  131.5 10.7 %collective-permute-start.19 = (bf16[2,2,64,512]{3,2,0,1:T(8,128)(2,1)}, bf16[2,2,64,512]{3,2,0,1:T(8,128)(2,1)S(1)}, u32[]{:S(2)}, u32[]{:S(2)}) collective-permute-start(bf16[2,2,64,512]{3,2,0,1:T(8,128)(2,1)} %fusion.56), channel_id=1, source_target_pairs={{0,16},{8,24},{16,0},{24,8},{1,17},{9,25},{17,1},{25,9},{2,18},{10... | collective-permute-start | bytes 786440 | tf_op jit(solution)/shard_map/ppermute | solution.py:45
  142.5 13.4 %collective-permute-start.25 = (f32[58,512]{1,0:T(8,128)S(1)}, f32[58,512]{1,0:T(8,128)S(1)}, u32[]{:S(2)}, u32[]{:S(2)}) collective-permute-start(f32[58,512]{1,0:T(8,128)S(1)} %add_add_fusion.1), channel_id=1, source_target_pairs={{0,1},{1,0},{2,3},{3,2},{4,5},{5,4},{6,7},{7,6},{8,9},{9,8},{10,11... | collective-permute-start | bytes 356360 | tf_op jit(solution)/shard_map/ppermute | solution.py:45
  144.3 11.7 %collective-permute-start.26 = (f32[58,512]{1,0:T(8,128)S(1)}, f32[58,512]{1,0:T(8,128)S(1)}, u32[]{:S(2)}, u32[]{:S(2)}) collective-permute-start(f32[58,512]{1,0:T(8,128)S(1)} %add_add_fusion.1), channel_id=1, source_target_pairs={{0,2},{1,3},{2,0},{3,1},{4,6},{5,7},{6,4},{7,5},{8,10},{9,11},{10,... | collective-permute-start | bytes 356360 | tf_op jit(solution)/shard_map/ppermute | solution.py:45
  146.2 9.7 %collective-permute-start.27 = (f32[58,512]{1,0:T(8,128)S(1)}, f32[58,512]{1,0:T(8,128)S(1)}, u32[]{:S(2)}, u32[]{:S(2)}) collective-permute-start(f32[58,512]{1,0:T(8,128)S(1)} %add_add_fusion.1), channel_id=1, source_target_pairs={{0,3},{1,2},{2,1},{3,0},{4,7},{5,6},{6,5},{7,4},{8,11},{9,10},{10,... | collective-permute-start | bytes 356360 | tf_op jit(solution)/shard_map/ppermute | solution.py:45
  146.2 10.1 %collective-permute-start.23 = (bf16[2,16,2048]{2,1,0:T(8,128)(2,1)S(1)}, bf16[2,16,2048]{2,1,0:T(8,128)(2,1)S(1)}, u32[]{:S(2)}, u32[]{:S(2)}) collective-permute-start(bf16[2,16,2048]{2,1,0:T(8,128)(2,1)S(1)} %fusion.57), channel_id=1, source_target_pairs={{0,2},{1,3},{2,0},{3,1},{4,6},{5,7},{6,4},{7,5},{8,10},{9,11},{10,... | collective-permute-start | bytes 393224 | tf_op jit(solution)/shard_map/ppermute | solution.py:45
  157.8 13.7 %collective-permute-start.30 = (f32[58,512]{1,0:T(8,128)S(1)}, f32[58,512]{1,0:T(8,128)S(1)}, u32[]{:S(2)}, u32[]{:S(2)}) collective-permute-start(f32[58,512]{1,0:T(8,128)S(1)} %add_add_fusion), channel_id=1, source_target_pairs={{0,4},{1,5},{2,6},{3,7},{4,0},{5,1},{6,2},{7,3},{8,12},{9,13},{10,... | collective-permute-start | bytes 356360 | tf_op jit(solution)/shard_map/ppermute | solution.py:45
  160.9 9.9 %collective-permute-start.28 = (bf16[16,2048]{1,0:T(8,128)(2,1)S(1)}, bf16[16,2048]{1,0:T(8,128)(2,1)S(1)}, u32[]{:S(2)}, u32[]{:S(2)}) collective-permute-start(bf16[16,2048]{1,0:T(8,128)(2,1)S(1)} %fusion.59), channel_id=1, source_target_pairs={{0,4},{1,5},{2,6},{3,7},{4,0},{5,1},{6,2},{7,3},{8,12},{9,13},{10,... | collective-permute-start | bytes 196616 | tf_op jit(solution)/shard_map/ppermute | solution.py:45
  161.0 10.5 %collective-permute-start.29 = (bf16[64,512]{1,0:T(8,128)(2,1)S(1)}, bf16[64,512]{1,0:T(8,128)(2,1)S(1)}, u32[]{:S(2)}, u32[]{:S(2)}) collective-permute-start(bf16[64,512]{1,0:T(8,128)(2,1)S(1)} %fusion.60), channel_id=1, source_target_pairs={{0,4},{1,5},{2,6},{3,7},{4,0},{5,1},{6,2},{7,3},{8,12},{9,13},{10,... | collective-permute-start | bytes 196616 | tf_op jit(solution)/shard_map/ppermute | solution.py:45
  (84 other events, 1131.8 us)
